TPU v7x, 32 devices: a whole 2x2x4 slice. The times are simulated.
32 devices in a mesh: groups: 2 (over x), replica: 4 (over z), tensor: 4 (over y, core).
Axes of the slice: x: 2, y: 2, z: 4, core: 2. Of those that a mesh axis runs over, the one named last changes fastest.
Arguments:
- queries: bfloat16 [2, 512, 8192], P(None, ('groups', 'replica'), 'tensor'), parts along dimension 1, may hold values from -6 to 6
- new_kv: bfloat16 [2, 512, 8, 256], P(None, ('groups', 'replica'), 'tensor'), parts along dimension 1, may hold values from -6 to 6, as said below
- pool: bfloat16 [5120, 16, 8, 256], P(('groups', 'replica'), None, 'tensor'), parts along dimension 0, may hold values from -6 to 6, as said below
- lengths: int32 [512], P(('groups', 'replica')), parts along dimension 0, may hold values from 0 to 160, as said below
- block_table: int32 [512, 10], P(('groups', 'replica')), parts along dimension 0, may hold values from 0 to 639, as said below
- plan: int32 [8, 4], P('groups'), parts along dimension 0, may hold values from 0 to 63, as said below
- w_out: bfloat16 [8192, 8192], P('tensor'), may hold values from -0.75 to 0.75
- residual: bfloat16 [2, 512, 8192], P(None, ('groups', 'replica')), parts along dimension 1, may hold values from -30 to 30
- norm_gain: bfloat16 [8192], replicated, may hold values from 0.099609375 to 1.8984375
Outputs:
- hidden: bfloat16 [2, 512, 8192], P(None, ('groups', 'replica')), parts along dimension 1
- normed: bfloat16 [2, 512, 8192], P(None, ('groups', 'replica')), parts along dimension 1
There are 2 independent parts, one for each index of `groups`. A program takes and returns all parts, laid end to end along the dimension named above; an argument that names none is the same for every part. Nothing has to cross between parts.
Inputs may be any that keep to these rules, and one draw needn't show every extreme that they name: `lengths`: 0 marks a free slot; a moved request of 160 tokens occurs in every draw. `plan`: half of the replicas are sources and half destinations; each source gives exactly 2 live requests, each destination takes exactly 2 into distinct free slots; no two rows share both source and destination. `block_table`: the first ceil(lengths[n] / 16) entries of a row are distinct blocks of the replica; the other entries are 0. `pool`: copies c and c' with c * 1 = c' * 8 // 8 are equal. `new_kv`: copies of one key-value head are equal, as in pool.
All inputs are finite; a program needn't handle non-finite values.
Results may differ from a plain program's by a relative error of at most 0.0062.
Values may be sent and summed in bfloat16 or wider, within the bound.
A program may use at most 192 MiB of HBM per device.

v0:
```python
import math

import jax
import jax.numpy as jnp
from jax import lax
from jax.sharding import PartitionSpec as P

SEND = 2


def attend(query_block, fresh_rows, cache_rows, live_count):
    head_dim = query_block.shape[-1]
    inv_root = 1.0 / math.sqrt(head_dim)
    past_keys = cache_rows[..., :head_dim]
    past_values = cache_rows[..., head_dim:]
    new_keys = fresh_rows[..., :head_dim]
    new_values = fresh_rows[..., head_dim:]
    past_scores = (
        jnp.einsum("snkgd,npkd->snkgp", query_block, past_keys, preferred_element_type=jnp.float32)
        * inv_root
    )
    fresh_scores = (
        jnp.einsum("snkgd,tnkd->snkgt", query_block, new_keys, preferred_element_type=jnp.float32)
        * inv_root
    )
    places = jnp.arange(cache_rows.shape[1], dtype=jnp.int32)
    seen = places[None, :] < live_count[:, None]
    past_scores = jnp.where(seen[None, :, None, None, :], past_scores, -jnp.inf)
    step_ids = jnp.arange(query_block.shape[0], dtype=jnp.int32)
    causal_mask = step_ids[:, None] >= step_ids[None, :]
    fresh_scores = jnp.where(causal_mask[:, None, None, None, :], fresh_scores, -jnp.inf)
    highest = jnp.maximum(jnp.max(past_scores, axis=-1), jnp.max(fresh_scores, axis=-1))
    past_exp = jnp.exp(past_scores - highest[..., None])
    fresh_exp = jnp.exp(fresh_scores - highest[..., None])
    denominator = jnp.sum(past_exp, axis=-1) + jnp.sum(fresh_exp, axis=-1)
    past_weights = (past_exp / denominator[..., None]).astype(jnp.bfloat16)
    fresh_weights = (fresh_exp / denominator[..., None]).astype(jnp.bfloat16)
    head_sum = jnp.einsum(
        "snkgp,npkd->snkgd", past_weights, past_values, preferred_element_type=jnp.float32
    )
    head_sum = head_sum + jnp.einsum(
        "snkgt,tnkd->snkgd", fresh_weights, new_values, preferred_element_type=jnp.float32
    )
    return head_sum.astype(jnp.bfloat16)


def finish(mixed_sum, resid_rows, keep_rows, gain_vector):
    full_sum = jnp.where(keep_rows[:, None], resid_rows.astype(jnp.float32) + mixed_sum, 0.0)
    hidden = full_sum.astype(jnp.bfloat16)
    widened = lax.optimization_barrier(hidden).astype(jnp.float32)
    mean_square = jnp.mean(widened * widened, axis=-1, keepdims=True)
    normed = (widened * lax.rsqrt(mean_square + 1e-05) * gain_vector.astype(jnp.float32)).astype(
        jnp.bfloat16
    )
    return (hidden, normed)


def per_device(queries, new_kv, pool, lengths, block_table, plan, w_out, residual, norm_gain):
    my_replica = lax.axis_index("replica")
    step_count = queries.shape[0]
    slot_count = lengths.shape[0]
    head_dim = pool.shape[3] // 2
    local_copies = pool.shape[2]
    local_heads = queries.shape[2] // head_dim
    group_size = local_heads // local_copies
    span = block_table.shape[1] * pool.shape[1]
    width = w_out.shape[1]
    source_slot = plan[:, 0]
    source = plan[:, 1]
    target = plan[:, 2]
    target_slot = plan[:, 3]
    plan_order = jnp.arange(plan.shape[0], dtype=jnp.int32)
    slot_ids = jnp.arange(slot_count, dtype=jnp.int32)
    sending = source == my_replica
    arriving = target == my_replica
    hit_in = arriving[None, :] & (target_slot[None, :] == slot_ids[:, None])
    incoming = jnp.any(hit_in, axis=1)
    moved_out = jnp.any(sending[None, :] & (source_slot[None, :] == slot_ids[:, None]), axis=1)
    live_rows = incoming | (lengths > 0) & jnp.logical_not(moved_out)
    query_block = queries.reshape(step_count, slot_count, local_copies, group_size, head_dim)
    own_cache = pool[block_table].reshape(slot_count, span, local_copies, 2 * head_dim)
    earlier = (source[None, :] == source[:, None]) & (plan_order[None, :] < plan_order[:, None])
    position = jnp.sum(earlier, axis=1)
    selector = sending[None, :] & (position[None, :] == jnp.arange(SEND, dtype=jnp.int32)[:, None])
    chosen = jnp.sum(jnp.where(selector, source_slot[None, :], 0), axis=1)
    present = jnp.any(selector, axis=1)
    blocks = pool[block_table[chosen]]
    sizes = jnp.where(present, lengths[chosen], 0)
    blocks, sizes = (blocks, sizes)
    got_blocks, got_sizes = (
        lax.all_gather(blocks, "replica", axis=0, tiled=True),
        lax.all_gather(sizes, "replica", axis=0, tiled=True),
    )
    where_from = source * SEND + position
    source_index = jnp.sum(jnp.where(hit_in, where_from[None, :], 0), axis=1)
    live_count = jnp.where(incoming, got_sizes[source_index], lengths)
    moved_cache = got_blocks[source_index].reshape(slot_count, span, local_copies, 2 * head_dim)
    cache_rows = jnp.where(incoming[:, None, None, None], moved_cache, own_cache)
    head_out = attend(query_block, new_kv, cache_rows, live_count)
    flat_heads = head_out.reshape(step_count * slot_count, local_heads * head_dim)
    keep_rows = jnp.tile(live_rows, step_count)
    resid_rows = residual.reshape(step_count * slot_count, width)
    mixed_sum = lax.psum(jnp.dot(flat_heads, w_out, preferred_element_type=jnp.float32), "tensor")
    hidden, normed = finish(mixed_sum, resid_rows, keep_rows, norm_gain)
    out_shape = (step_count, slot_count, width)
    return (hidden.reshape(out_shape), normed.reshape(out_shape))


def solution(mesh):
    in_specs = (
        P(None, ("groups", "replica"), "tensor"),
        P(None, ("groups", "replica"), "tensor", None),
        P(("groups", "replica"), None, "tensor", None),
        P(("groups", "replica")),
        P(("groups", "replica"), None),
        P("groups", None),
        P("tensor", None),
        P(None, ("groups", "replica"), None),
        P(),
    )
    out_specs = (P(None, ("groups", "replica"), None), P(None, ("groups", "replica"), None))
    return jax.shard_map(
        per_device, mesh=mesh, in_specs=in_specs, out_specs=out_specs, check_vma=False
    )
```

profile of v0, /device:TPU:0, one launch (start us, length us, event | category | flops | bytes accessed | tf_op | source)
XLA Modules:
  0.0 222.7 jit_solution(18025069852136357616)
XLA Ops:
  7.2 0.0 all-gather.3.cloned.1.call-start
  7.2 0.8 copy.48
  8.0 1.0 slice_reduce_fusion.2
  9.0 0.2 convert_reduce_fusion
  9.2 0.1 select_reduce_fusion.1
  9.3 0.6 gather_fusion
  9.9 0.1 reshape.156
  10.0 5.2 %gather_fusion.1 = bf16[20,16,2,256]{3,2,1,0:T(2,128)(2,1)S(1)} fusion(bf16[640,16,2,256]{3,2,1,0:T(2,128)(2,1)} %param.11, s32[1024]{0:T(1024)S(1)} %pad_clamp_fusion.2), kind=kCustom, calls=%fused_computation.1 | custom fusion | bytes 655440 | tf_op jit(solution)/shard_map/gather | solution.py:87
  15.2 0.8 copy.49
  16.0 0.0 all-reduce.3.cloned.1.call-start
  16.0 0.7 compare_select_fusion
  16.7 0.1 fusion.30
  16.9 0.1 copy.51
  17.0 0.1 reshape.172
  17.1 1.3 gather_fusion.4
  18.4 1.2 dynamic-slice
  20.3 0.1 select_dynamic-update-slice_fusion
  20.4 10.0 %all-reduce = s32[8]{0:T(128)S(1)} all-reduce(s32[8]{0:T(128)S(1)} %select_dynamic-update-slice_fusion), channel_id=1, replica_groups=mesh['groups'=2,'replica'=4,'tensor'=4] {'replica'}, use_global_device_ids=true, to_apply=%add | all-reduce | flops 8 | bytes 64
  30.5 36.4 %gather_fusion.3 = bf16[640,16,2,256]{3,2,1,0:T(2,128)(2,1)} fusion(bf16[640,16,2,256]{3,2,1,0:T(2,128)(2,1)} %param.11, s32[1024]{0:T(1024)S(1)} %pad_clamp_fusion), kind=kCustom, calls=%fused_computation.3 | custom fusion | bytes 20974080 | tf_op jit(solution)/shard_map/gather | solution.py:81
  66.9 0.1 copy.67
  67.0 0.2 fusion.24
  67.2 0.1 select_reduce_fusion
  67.3 0.7 fusion.37
  68.0 0.1 fusion.29
  68.1 5.0 %fusion.31 = s32[64]{0:T(128)S(1)} fusion(pred[64]{0:T(512)(128)(4,1)S(1)} %fusion.29, s32[64]{0:T(128)S(1)} %copy-done, s32[]{:T(128)} %bitcast.12, s32[]{:T(128)} %bitcast.13, s32[]{:T(128)} %bitcast.14, s32[]{:T(128)} %bitcast.15, s32[]{:T(128)} %bitcast.16, s32[]{:T(128)} %bitcast.17, s32[]{:T(128)} %bitcast.18, s32[]{:T(128)} %bitcast.19, ...), kind=kLoop, calls=%fused_computation.81 | loop fusion | flops 1152 | bytes 864 | tf_op jit(solution)/shard_map/jit(_where)/select_n | solution.py:96
  73.0 0.1 iota_compare_fusion
  73.1 0.1 fusion.36
  73.2 2.4 %fusion.38 = (f32[2,64,2,8]{3,0,2,1:T(2,128)S(1)}, f32[2,64,2,8,2]{3,4,0,2,1:T(2,128)S(1)}) fusion(bf16[2,64,2,8,128]{4,3,2,1,0:T(8,128)(2,1)S(1)} %bitcast.95, bf16[2,64,2,128]{3,2,1,0:T(2,128)(2,1)S(1)} %get-tuple-element.6, pred[2,2]{1,0:T(4,128)(4,1)S(1)} %iota_compare_fusion.4), kind=kOutput, calls=%fused_computation.92 | convolution fusion | flops 1058816 | bytes 614404 | tf_op jit(solution)/shard_map/snkgd,tnkd->snkgt/dot_general | solution.py:23
  75.7 7.3 %gather_fusion.2 = bf16[64,10,16,2,256]{4,2,3,1,0:T(8,128)(2,1)} fusion(bf16[8,10,16,2,256]{4,2,3,1,0:T(8,128)(2,1)} %all-gather.3.cloned.1.call-done, s32[1024]{0:T(1024)S(1)} %pad_clamp_fusion.1), kind=kCustom, calls=%fused_computation.2 | custom fusion | bytes 20971776 | tf_op jit(solution)/shard_map/gather | solution.py:97
  83.0 9.3 %copy.50 = bf16[64,10,16,2,256]{4,2,1,3,0:T(8,128)(2,1)} copy(bf16[64,10,16,2,256]{4,2,3,1,0:T(8,128)(2,1)} %gather_fusion.2) | data formatting | bytes 20971520 | tf_op jit(solution)/shard_map/gather | solution.py:97
  92.3 8.7 %copy_select_fusion = bf16[64,160,2,256]{3,1,2,0:T(8,128)(2,1)S(1)} fusion(bf16[64,160,2,256]{3,2,1,0:T(2,128)(2,1)} %bitcast.90, bf16[64,10,16,2,256]{4,2,1,3,0:T(8,128)(2,1)} %copy.50, pred[64]{0:T(512)(128)(4,1)S(1)} %fusion.29), kind=kLoop, calls=%fused_computation.5 | loop fusion | flops 5242880 | bytes 31457344 | tf_op jit(solution)/shard_map/jit(_where)/select_n | solution.py:98
  101.0 3.0 %bitcast_reduce_fusion = (f32[2,64,2,8]{3,0,2,1:T(2,128)S(1)}, f32[64,2,160,2,8]{2,4,3,1,0:T(8,128)S(1)}) fusion(pred[64,160]{1,0:T(8,128)(4,1)S(1)} %iota_compare_fusion, bf16[2,64,2,8,128]{4,3,2,1,0:T(8,128)(2,1)S(1)} %bitcast.96, bf16[64,160,2,256]{3,1,2,0:T(8,128)(2,1)S(1)} %copy_select_fusion), kind=kOutput, calls=%fused_computation.19 | convolution fusion | flops 84867072 | bytes 7102464 | tf_op jit(solution)/shard_map/snkgd,npkd->snkgp/dot_general | solution.py:19
  104.0 0.1 max.7
  104.1 1.1 fusion.8
  105.2 0.5 fusion.21
  105.7 0.1 add.77
  105.8 1.9 fusion.9
  107.7 0.5 fusion.11
  108.3 0.1 copy.58
  108.4 0.2 reshape.142
  108.6 17.1 %fusion.39 = f32[128,8192]{1,0:T(8,128)} fusion(bf16[128,2048]{1,0:T(8,128)(2,1)S(1)} %reshape.142, bf16[2048,8192]{1,0:T(8,128)(2,1)} %param.15), kind=kOutput, calls=%fused_computation.93 | convolution fusion | flops 4294967296 | bytes 38273024 | tf_op jit(solution)/shard_map/dot_general | solution.py:103
  125.7 0.1 fusion.27
  125.8 0.1 broadcast_in_dim.70
  125.9 0.5 copy-done.6
  126.4 84.2 %all-reduce.3.cloned.1.call-done = f32[128,8192]{1,0:T(8,128)} async-done(((f32[128,8192]{1,0:T(8,128)}), f32[128,8192]{1,0:T(8,128)}) %all-reduce.3.cloned.1.call-update) | async-done | bytes 4194320 | tf_op jit(solution)/shard_map/psum | solution.py:103
  210.6 2.8 %fusion.6 = bf16[128,8192]{1,0:T(8,128)(2,1)S(1)} fusion(f32[128,8192]{1,0:T(8,128)} %all-reduce.3.cloned.1.call-done, bf16[2,64,8192]{2,1,0:T(8,128)(2,1)S(1)} %copy-done.2, pred[128]{0:T(512)(128)(4,1)S(1)} %broadcast_in_dim.70), kind=kLoop, calls=%fused_computation.17 | loop fusion | flops 4194304 | bytes 8388736 | tf_op jit(solution)/shard_map/convert_element_type | solution.py:49
  213.4 0.5 fusion.2
  213.9 2.0 fusion.4
  (31 shorter events, 0.2 us)
Async XLA Ops:
  7.2 68.5 %all-gather.3.cloned.1.call-start = ((), (), s32[]{:S(2)}) async-start(), calls=%async_computation.1 | async-start | bytes 1638400 | tf_op jit(solution)/shard_map/all_gather | solution.py:91
  16.0 194.6 %all-reduce.3.cloned.1.call-start = ((), (), s32[]{:S(2)}) async-start(), calls=%async_computation | async-start | bytes 8388608 | tf_op jit(solution)/shard_map/psum | solution.py:103
  30.4 36.5 %copy-start.3 = (bf16[2,64,2048]{2,1,0:T(8,128)(2,1)S(1)}, bf16[2,64,2048]{2,1,0:T(8,128)(2,1)}, u32[]{:S(2)}) copy-start(bf16[2,64,2048]{2,1,0:T(8,128)(2,1)} %param.9) | copy-start | bytes 1572868
  30.4 36.6 %copy-start.5 = (s32[4,4]{1,0:T(4,128)S(1)}, s32[4,4]{1,0:T(4,128)}, u32[]{:S(2)}) copy-start(s32[4,4]{1,0:T(4,128)} %param.14) | copy-start | bytes 196
  30.4 37.6 %copy-start = (s32[64]{0:T(128)S(1)}, s32[64]{0:T(128)}, u32[]{:S(2)}) copy-start(s32[64]{0:T(128)} %param.12) | copy-start | bytes 772
  30.4 42.7 %copy-start.4 = (bf16[2,64,2,256]{3,2,1,0:T(2,128)(2,1)S(1)}, bf16[2,64,2,256]{3,2,1,0:T(2,128)(2,1)}, u32[]{:S(2)}) copy-start(bf16[2,64,2,256]{3,2,1,0:T(2,128)(2,1)} %param.10) | copy-start | bytes 393220
  125.7 0.7 copy-start.6
  125.7 84.9 %copy-start.2 = (bf16[2,64,8192]{2,1,0:T(8,128)(2,1)S(1)}, bf16[2,64,8192]{2,1,0:T(8,128)(2,1)}, u32[]{:S(2)}) copy-start(bf16[2,64,8192]{2,1,0:T(8,128)(2,1)} %param.16) | copy-start | bytes 6291460
  213.4 2.5 %copy-start.1 = (bf16[128,8192]{1,0:T(8,128)(2,1)}, bf16[128,8192]{1,0:T(8,128)(2,1)S(1)}, u32[]{:S(2)}) copy-start(bf16[128,8192]{1,0:T(8,128)(2,1)S(1)} %fusion.6) | copy-start | bytes 6291460
Sparse Core Ops, SparseCore 0:
  16.1 35.5 all-gather.2
  125.8 84.7 all-reduce.2
where the time goes:
time: 223 us
  waiting for transfers between devices  84.3 us (38%)
  local copies, waits for them, and re-layouts  66 us (30%)
  matrix products  24.9 us (11%)
  other arithmetic  22.5 us (10%)
  between operations  14.9 us (7%)
  blocking collectives  10 us (4%)
    psum x1, waiting for transfers between devices, per_device(): lax.psum(jnp.dot(flat_heads, w_out, preferred_element_type=jnp.float32),...  84.2 us
    gather x1, local copies, waits for them, and re-layouts, per_device(): pool[block_table].reshape(slot_count, span, local_copies, 2 * head_dim)  36.4 us
    dot_general x1, matrix products, per_device(): jnp.dot(flat_heads, w_out, preferred_element_type=jnp.float32)  17.1 us
    gather x2, local copies, waits for them, and re-layouts, per_device(): got_blocks[source_index]  16.6 us
    unnamed x1, blocking collectives  10 us
    select_n x1, other arithmetic, per_device(): jnp.where(incoming[:, None, None, None], moved_cache, own_cache)  8.72 us
    gather x3, local copies, waits for them, and re-layouts, per_device(): blocks = pool[block_table[chosen]]  6.51 us
    select_n x1, other arithmetic, per_device(): live_count = jnp.where(incoming, got_sizes[source_index], lengths)  4.95 us
  transfers between devices with their start and end apart: 2, of which 1 were waited for; matrix products, arithmetic and copies ran while one was open for 22% of the time, Pallas kernels for 0%

commit v1 on v0

v1 whole, which is shorter than its diff:
```python
import functools
import math

import jax
import jax.numpy as jnp
from jax import lax
from jax.experimental import pallas as pl
from jax.experimental.pallas import tpu as pltpu
from jax.sharding import PartitionSpec as P

SEND = 2
CHUNK = 512
MESH = pl.DeviceIdType.MESH
VMEM = pl.BlockSpec(memory_space=pltpu.VMEM)
ANY = pl.BlockSpec(memory_space=pl.ANY)
SMEM = pl.BlockSpec(memory_space=pltpu.SMEM)


def attend_kernel(dims, table_ref, count_ref, query_ref, fresh_ref, pool_ref, out_ref, keys, values, sems):
    slots, blocks, steps, heads, copies, unroll = dims
    head_dim = query_ref.shape[-1]
    rows = steps * heads
    block_rows = keys.shape[1] * copies
    cached = blocks * block_rows
    fresh_pad = fresh_ref.shape[1]
    total = cached + fresh_pad
    get_keys = pltpu.make_async_copy(pool_ref.at[..., pl.ds(0, head_dim)], keys, sems.at[0])
    get_values = pltpu.make_async_copy(pool_ref.at[..., pl.ds(head_dim, head_dim)], values, sems.at[1])
    get_keys.start()
    get_values.start()
    inv_root = 1.0 / math.sqrt(head_dim)
    row = lax.broadcasted_iota(jnp.int32, (rows, total), 0)
    col = lax.broadcasted_iota(jnp.int32, (rows, total), 1)
    step = row // heads
    copy = (row % heads) // (heads // copies)
    is_fresh = col >= cached
    fresh_step = (col - cached) // copies
    same_copy = (col % copies) == copy
    fresh_ok = is_fresh & same_copy & (fresh_step <= step)
    old_limit = jnp.where(is_fresh | jnp.logical_not(same_copy), 1 << 20, col)
    get_keys.wait()
    get_values.wait()

    def one(n):
        kk = [keys[table_ref[n * blocks + b]].reshape(block_rows, head_dim) for b in range(blocks)]
        vv = [values[table_ref[n * blocks + b]].reshape(block_rows, head_dim) for b in range(blocks)]
        new = fresh_ref[n]
        kk = jnp.concatenate(kk + [new[:, :head_dim]], axis=0)
        vv = jnp.concatenate(vv + [new[:, head_dim:]], axis=0)
        scores = lax.dot_general(
            query_ref[n], kk, (((1,), (1,)), ((), ())), preferred_element_type=jnp.float32
        ) * inv_root
        ok = fresh_ok | (old_limit < count_ref[n] * copies)
        scores = jnp.where(ok, scores, -jnp.inf)
        top = jnp.max(scores, axis=-1, keepdims=True)
        powers = jnp.exp(scores - top)
        denominator = jnp.sum(powers, axis=-1, keepdims=True)
        weights = (powers / denominator).astype(jnp.bfloat16)
        out_ref[n] = jnp.dot(weights, vv, preferred_element_type=jnp.float32).astype(jnp.bfloat16)

    def body(i, carry):
        for u in range(unroll):
            one(i * unroll + u)
        return carry

    lax.fori_loop(0, slots // unroll, body, 0)


def attend(query_rows, fresh_rows, pool, table, count, steps, copies):
    slots, rows, head_dim = query_rows.shape
    blocks = table.shape[1]
    if copies == 1:
        pool = pool.reshape(pool.shape[0], pool.shape[1], pool.shape[3])
    unroll = 4 if slots % 4 == 0 else 1
    dims = (slots, blocks, steps, rows // steps, copies, unroll)
    part = pool.shape[:-1] + (head_dim,)
    return pl.pallas_call(
        functools.partial(attend_kernel, dims),
        out_shape=jax.ShapeDtypeStruct((slots, rows, head_dim), jnp.bfloat16),
        in_specs=[SMEM, SMEM, VMEM, VMEM, ANY],
        out_specs=VMEM,
        scratch_shapes=[
            pltpu.VMEM(part, jnp.bfloat16),
            pltpu.VMEM(part, jnp.bfloat16),
            pltpu.SemaphoreType.DMA((2,)),
        ],
        compiler_params=pltpu.CompilerParams(vmem_limit_bytes=40 * 2**20),
        cost_estimate=pl.CostEstimate(
            flops=4 * slots * rows * 336 * head_dim, bytes_accessed=4 * pool.size, transcendentals=slots * rows * 336
        ),
    )(table.reshape(-1), count, query_rows, fresh_rows, pool)


def pack_kernel(blocks, table_ref, chosen_ref, size_ref, pool_ref, out_ref, note, sems):
    copies = []
    for j in range(SEND):
        for b in range(blocks):
            copies.append(
                pltpu.make_async_copy(
                    pool_ref.at[table_ref[chosen_ref[j] * blocks + b]],
                    out_ref.at[j * (blocks + 1) + b],
                    sems.at[j * (blocks + 1) + b],
                )
            )
            copies[-1].start()
    for j in range(SEND):
        size = jnp.full(note.shape[1:], size_ref[j], jnp.int32)
        note[j] = size.astype(jnp.float32).astype(jnp.bfloat16)
        at = j * (blocks + 1) + blocks
        copies.append(pltpu.make_async_copy(note.at[j], out_ref.at[at], sems.at[at]))
        copies[-1].start()
    for copy in copies:
        copy.wait()


def pack(pool, table, chosen, sizes):
    blocks = table.shape[1]
    count = SEND * (blocks + 1)
    return pl.pallas_call(
        functools.partial(pack_kernel, blocks),
        out_shape=jax.ShapeDtypeStruct((count,) + pool.shape[1:], pool.dtype),
        in_specs=[SMEM, SMEM, SMEM, ANY],
        out_specs=ANY,
        scratch_shapes=[
            pltpu.VMEM((SEND,) + pool.shape[1:], pool.dtype),
            pltpu.SemaphoreType.DMA((count,)),
        ],
    )(table.reshape(-1), chosen, sizes, pool)


def project_kernel(ranks, head_ref, keep_ref, gain_ref, resid_ref, w_ref, hidden_ref, normed_ref,
                   weight, sib_out, sib_in, y_out, y_in, whole, w_sem, s_send, s_recv, y_send, y_recv,
                   g_send, g_recv, h_send, h_recv):
    rows, width = hidden_ref.shape
    tall = ranks // 2
    pieces = width // ranks // CHUNK
    me = lax.axis_index("tensor")
    level = me // 2
    core = me % 2
    sibling = level * 2 + 1 - core

    def place(side, at_level, k):
        return (side * tall + at_level) * pieces + k

    def peer(off):
        return lax.rem(level + off, tall) * 2 + core

    barrier = pltpu.get_barrier_semaphore()
    pl.semaphore_signal(barrier, inc=1, device_id={"tensor": sibling}, device_id_type=MESH)
    for off in range(1, tall):
        pl.semaphore_signal(barrier, inc=1, device_id={"tensor": peer(off)}, device_id_type=MESH)

    def fetch(i, side):
        at_level = lax.rem(level + 1 + i // pieces, tall)
        chunk = place(side, at_level, lax.rem(i, pieces))
        slot = i * 2 + (0 if side is sib_side else 1)
        return pltpu.make_async_copy(
            w_ref.at[:, pl.ds(pl.multiple_of(chunk * CHUNK, CHUNK), CHUNK)], weight.at[slot], w_sem.at[slot]
        )

    sib_side = 1 - core
    steps = tall * pieces

    def start_fetch(i, carry):
        fetch(i, sib_side).start()
        fetch(i, core).start()
        return carry

    lax.fori_loop(0, steps, start_fetch, 0)
    pl.semaphore_wait(barrier, tall)

    def to_sibling(i):
        return pltpu.make_async_remote_copy(
            sib_out.at[i], sib_in.at[i], s_send.at[i], s_recv.at[i],
            device_id={"tensor": sibling}, device_id_type=MESH)

    def to_peer(i):
        off = 1 + i // pieces
        return pltpu.make_async_remote_copy(
            y_out.at[i], y_in.at[i], y_send.at[i], y_recv.at[i],
            device_id={"tensor": peer(off)}, device_id_type=MESH)

    def gather_peer(off, k):
        at = (off - 1) * pieces + k
        slot = place(core, level, k)
        return pltpu.make_async_remote_copy(
            whole.at[slot], whole.at[slot], g_send.at[at], g_recv.at[at],
            device_id={"tensor": peer(off)}, device_id_type=MESH)

    def gather_wait(off, k):
        at = (off - 1) * pieces + k
        slot = place(core, lax.rem(level + tall - off, tall), k)
        return slot, pltpu.make_async_remote_copy(
            whole.at[slot], whole.at[slot], g_send.at[at], g_recv.at[at],
            device_id={"tensor": peer(off)}, device_id_type=MESH)

    def hand_over(side, off, k):
        at = off * pieces + k
        slot = place(side, lax.rem(level + tall - off, tall), k)
        return slot, pltpu.make_async_remote_copy(
            whole.at[slot], whole.at[slot], h_send.at[at], h_recv.at[at],
            device_id={"tensor": sibling}, device_id_type=MESH)

    def products(i):
        fetch(i, sib_side).wait()
        sib_out[i] = jnp.dot(
            head_ref[...], weight[i * 2], preferred_element_type=jnp.float32
        ).astype(jnp.bfloat16)
        to_sibling(i).start()
        fetch(i, core).wait()
        mine = jnp.dot(head_ref[...], weight[i * 2 + 1], preferred_element_type=jnp.float32)
        to_sibling(i).wait_recv()
        return mine + sib_in[i].astype(jnp.float32)

    def far(i, carry):
        y_out[i] = products(i).astype(jnp.bfloat16)
        to_peer(i).start()
        return carry

    lax.fori_loop(0, steps - pieces, far, 0)

    def near(k, carry):
        mixed = products(steps - pieces + k)
        for off in range(1, tall):
            at = (off - 1) * pieces + k
            to_peer(at).wait_recv()
            mixed = mixed + y_in[at].astype(jnp.float32)
        slot = place(core, level, k)
        cols = pl.ds(pl.multiple_of(slot * CHUNK, CHUNK), CHUNK)
        total = resid_ref[:, cols].astype(jnp.float32) + mixed
        whole[slot] = jnp.where(keep_ref[...] > 0.0, total, 0.0).astype(jnp.bfloat16)
        for off in range(1, tall):
            gather_peer(off, k).start()
        hand_over(core, 0, k)[1].start()
        return carry

    lax.fori_loop(0, pieces, near, 0)

    def square(slot):
        wide = whole[slot].astype(jnp.float32)
        return jnp.sum(wide * wide, axis=-1, keepdims=True)

    squares = jnp.zeros((rows, 1), jnp.float32)
    for k in range(pieces):
        squares = squares + square(place(core, level, k))
        slot, copy = hand_over(sib_side, 0, k)
        copy.wait_recv()
        squares = squares + square(slot)
    for k in range(pieces):
        for off in range(1, tall):
            slot, copy = gather_wait(off, k)
            copy.wait_recv()
            hand_over(core, off, k)[1].start()
            squares = squares + square(slot)
    for k in range(pieces):
        for off in range(1, tall):
            slot, copy = hand_over(sib_side, off, k)
            copy.wait_recv()
            squares = squares + square(slot)
    scale = lax.rsqrt(squares * (1.0 / width) + 1e-05)
    for j in range(width // CHUNK):
        cols = pl.ds(j * CHUNK, CHUNK)
        hidden = whole[j]
        hidden_ref[:, cols] = hidden
        normed_ref[:, cols] = (hidden.astype(jnp.float32) * scale * gain_ref[:, cols]).astype(jnp.bfloat16)
    for i in range(steps):
        to_sibling(i).wait_send()
    for i in range(steps - pieces):
        to_peer(i).wait_send()
    for k in range(pieces):
        hand_over(core, 0, k)[1].wait_send()
        for off in range(1, tall):
            gather_peer(off, k).wait_send()
            hand_over(core, off, k)[1].wait_send()


def project(flat_heads, keep_rows, gain, resid_rows, w_out, ranks):
    rows = flat_heads.shape[0]
    depth, width = w_out.shape
    pieces = width // ranks // CHUNK
    steps = ranks // 2 * pieces
    far = steps - pieces
    block = (rows, CHUNK)
    dma = pltpu.SemaphoreType.DMA
    out = jax.ShapeDtypeStruct((rows, width), jnp.bfloat16)
    return pl.pallas_call(
        functools.partial(project_kernel, ranks),
        out_shape=(out, out),
        in_specs=[VMEM, VMEM, VMEM, VMEM, ANY],
        out_specs=(VMEM, VMEM),
        scratch_shapes=[
            pltpu.VMEM((2 * steps, depth, CHUNK), jnp.bfloat16),
            pltpu.VMEM((steps,) + block, jnp.bfloat16),
            pltpu.VMEM((steps,) + block, jnp.bfloat16),
            pltpu.VMEM((far,) + block, jnp.bfloat16),
            pltpu.VMEM((far,) + block, jnp.bfloat16),
            pltpu.VMEM((2 * steps,) + block, jnp.bfloat16),
            dma((2 * steps,)),
            dma((steps,)), dma((steps,)),
            dma((far,)), dma((far,)),
            dma((far,)), dma((far,)),
            dma((steps,)), dma((steps,)),
        ],
        compiler_params=pltpu.CompilerParams(
            collective_id=0, has_side_effects=True, vmem_limit_bytes=56 * 2**20
        ),
        cost_estimate=pl.CostEstimate(
            flops=2 * rows * depth * width, bytes_accessed=2 * depth * width, transcendentals=0
        ),
    )(flat_heads, keep_rows, gain, resid_rows, w_out)


def per_device(ranks, queries, new_kv, pool, lengths, block_table, plan, w_out, residual, norm_gain):
    my_replica = lax.axis_index("replica")
    steps, slots, _ = queries.shape
    head_dim = pool.shape[3] // 2
    copies = pool.shape[2]
    heads = queries.shape[2] // head_dim
    blocks = block_table.shape[1]
    width = w_out.shape[1]
    source_slot, source, target, target_slot = (plan[:, i] for i in range(4))
    order = jnp.arange(plan.shape[0], dtype=jnp.int32)
    slot_ids = jnp.arange(slots, dtype=jnp.int32)
    ranks_of = jnp.arange(SEND, dtype=jnp.int32)
    sending = source == my_replica
    arriving = target == my_replica
    before = order[None, :] < order[:, None]
    position = jnp.sum((source[None, :] == source[:, None]) & before, axis=1)
    selector = sending[None, :] & (position[None, :] == ranks_of[:, None])
    chosen = jnp.sum(jnp.where(selector, source_slot[None, :], 0), axis=1)
    sizes = jnp.sum(jnp.where(slot_ids[None, :] == chosen[:, None], lengths[None, :], 0), axis=1)
    got = lax.all_gather(pack(pool, block_table, chosen, sizes), "replica", axis=0, tiled=True)

    query_rows = queries.reshape(steps, slots, heads, head_dim).transpose(1, 0, 2, 3)
    query_rows = query_rows.reshape(slots, steps * heads, head_dim)
    fresh_rows = new_kv.transpose(1, 0, 2, 3).reshape(slots, steps * copies, 2 * head_dim)
    fresh_rows = jnp.pad(fresh_rows, ((0, 0), (0, 16 - steps * copies), (0, 0)))
    main = attend(query_rows, fresh_rows, pool, block_table, lengths, steps, copies)

    turn = jnp.sum((target[None, :] == target[:, None]) & before, axis=1)
    arrival = arriving[None, :] & (turn[None, :] == ranks_of[:, None])
    from_index = jnp.sum(jnp.where(arrival, (source * SEND + position)[None, :], 0), axis=1)
    to_slot = jnp.sum(jnp.where(arrival, target_slot[None, :], 0), axis=1)
    to_slot = jnp.where(jnp.any(arrival, axis=1), to_slot, -1)
    got_sizes = got[blocks :: blocks + 1, 0, 0, 0].astype(jnp.int32)
    moved_hit = jnp.arange(got_sizes.shape[0], dtype=jnp.int32)[None, :] == from_index[:, None]
    moved_count = jnp.sum(jnp.where(moved_hit, got_sizes[None, :], 0), axis=1)
    moved_table = from_index[:, None] * (blocks + 1) + jnp.arange(blocks, dtype=jnp.int32)[None, :]
    pick = jnp.maximum(to_slot, 0)
    extra = attend(query_rows[pick], fresh_rows[pick], got, moved_table, moved_count, steps, copies)
    head_out = main
    for j in range(SEND):
        head_out = jnp.where((slot_ids == to_slot[j])[:, None, None], extra[j][None], head_out)
    flat_heads = head_out.reshape(slots, steps, heads * head_dim).transpose(1, 0, 2)
    flat_heads = flat_heads.reshape(steps * slots, heads * head_dim)

    incoming = jnp.any(arriving[None, :] & (target_slot[None, :] == slot_ids[:, None]), axis=1)
    moved_out = jnp.any(sending[None, :] & (source_slot[None, :] == slot_ids[:, None]), axis=1)
    live = incoming | (lengths > 0) & jnp.logical_not(moved_out)
    keep_rows = jnp.tile(live, steps)[:, None].astype(jnp.float32)
    gain = norm_gain.astype(jnp.float32)[None, :]
    resid_rows = residual.reshape(steps * slots, width)
    hidden, normed = project(flat_heads, keep_rows, gain, resid_rows, w_out, ranks)
    out_shape = (steps, slots, width)
    return (hidden.reshape(out_shape), normed.reshape(out_shape))


def solution(mesh):
    in_specs = (
        P(None, ("groups", "replica"), "tensor"),
        P(None, ("groups", "replica"), "tensor", None),
        P(("groups", "replica"), None, "tensor", None),
        P(("groups", "replica")),
        P(("groups", "replica"), None),
        P("groups", None),
        P("tensor", None),
        P(None, ("groups", "replica"), None),
        P(),
    )
    out_specs = (P(None, ("groups", "replica"), None), P(None, ("groups", "replica"), None))
    return jax.shard_map(
        functools.partial(per_device, mesh.shape["tensor"]),
        mesh=mesh, in_specs=in_specs, out_specs=out_specs, check_vma=False,
    )
```

time: 223 us -> 122 us (0.55)
  waiting for transfers between devices: 84.3 us -> 0.04 us
  Pallas kernels: 0 us -> 81.5 us
  local copies, waits for them, and re-layouts: 66 us -> 19.9 us
  matrix products: 24.9 us -> 0 us
  other arithmetic: 22.5 us -> 5.48 us
  blocking collectives: 10 us -> 0 us
    psum x1 -> x0, waiting for transfers between devices: 84.2 us -> none  [per_device(): lax.psum(jnp.dot(flat_heads, w_out, preferred_element_type=jnp.float32),...]
    pallas_call x0 -> x4, Pallas kernels: none -> 81.5 us  [the longest x1 36.1 us: project(): pl.pallas_call(functools.partial(project_kernel, ranks), out_shape=(out,...]
    gather x8 -> x3, local copies, waits for them, and re-layouts: 61.5 us -> 1.14 us  [the longest x2 0.58 us: per_device(): fresh_rows[pick]]
    dot_general x5 -> x0, matrix products: 24.9 us -> none  [the longest x1 17.1 us: per_device(): jnp.dot(flat_heads, w_out, preferred_element_type=jnp.float32)]
    select_n x6 -> x1, other arithmetic: 14.4 us -> 0.21 us  [per_device(): jnp.where((slot_ids == to_slot[j])[:, None, None], extra[j][None], head_out)]
    unnamed x1 -> x0, blocking collectives: 10 us -> none
    unnamed x18 -> x20, local copies, waits for them, and re-layouts: 2.66 us -> 9.47 us
    convert_element_type x3 -> x2, other arithmetic: 4.76 us -> 0.96 us  [the longest x1 0.96 us: per_device(): got_sizes = got[blocks::blocks + 1, 0, 0, 0].astype(jnp.int32)]
  transfers between devices with their start and end apart: 2 -> 1, of which waited for: 1 -> 0; matrix products, arithmetic and copies ran while one was open for 22% -> 4% of each run, Pallas kernels for 0% -> 25%
where the time goes in v1:
time: 122 us; the launch traced here: 121 us
  Pallas kernels  81.5 us (67%)
  local copies, waits for them, and re-layouts  19.9 us (16%)
  between operations  14.3 us (12%)
  other arithmetic  5.48 us (4%)
    pallas_call x1, Pallas kernels, project(): pl.pallas_call(functools.partial(project_kernel, ranks), out_shape=(out,...  36.1 us
    pallas_call x2, Pallas kernels, attend(): pl.pallas_call(functools.partial(attend_kernel, dims), out_shape=jax.Shap...  33.3 us
    pallas_call x1, Pallas kernels, pack(): pl.pallas_call(functools.partial(pack_kernel, blocks), out_shape=jax.Shap...  12.1 us
    unnamed x20, local copies, waits for them, and re-layouts  9.47 us
    all_gather x1, local copies, waits for them, and re-layouts, per_device(): lax.all_gather(pack(pool, block_table, chosen, sizes), 'replica', axis=0,...  2.94 us
  transfers between devices with their start and end apart: 1, of which 0 were waited for; matrix products, arithmetic and copies ran while one was open for 4% of the time, Pallas kernels for 25%

profile of v1, /device:TPU:0, one launch (start us, length us, event | category | flops | bytes accessed | tf_op | source)
XLA Modules:
  0.0 121.2 jit_solution(8672802106254890872)
XLA Ops:
  7.2 0.0 all-gather.2.cloned.1.call-start
  7.2 1.0 slice_reduce_fusion
  8.3 0.2 convert_reduce_fusion.1
  8.5 0.8 copy.27
  9.3 0.7 reshape.114.table_ref
  10.0 0.1 fusion.7.chosen_ref
  10.1 1.4 %fusion.8.size_ref = s32[2]{0:T(128)} fusion(s32[64]{0:T(128)} %count_ref.1, s32[2]{0:T(128)S(1)} %fusion.7.chosen_ref), kind=kLoop, calls=%fused_computation.29 | loop fusion | flops 382 | bytes 272 | tf_op jit(solution)/shard_map/reduce_sum | solution.py:331
  11.6 0.0 copy-done.7
  11.6 12.1 %shard_map.104 = bf16[22,16,2,256]{3,2,1,0:T(2,128)(2,1)} custom-call(s32[640]{0:T(1024)} %reshape.114.table_ref, s32[2]{0:T(128)} %copy-done.7, s32[2]{0:T(128)} %fusion.8.size_ref, bf16[640,16,2,256]{3,2,1,0:T(2,128)(2,1)} %pool_ref.3), custom_call_target="tpu_custom_call" | custom-call | tf_op jit(solution)/shard_map/pallas_call | solution.py:119
  23.7 0.0 copy-start.4
  23.7 1.8 %copy.28 = bf16[22,16,2,256]{3,1,2,0:T(8,128)(2,1)} copy(bf16[22,16,2,256]{3,2,1,0:T(2,128)(2,1)} %shard_map.104) | data formatting | bytes 720896 | tf_op jit(solution)/shard_map/pallas_call | solution.py:119
  25.5 0.0 all-gather.2.cloned.1.call-update
  25.6 0.1 select_reduce_fusion
  25.7 0.1 iota_add_fusion
  25.8 0.1 add.34.table_ref
  25.9 0.0 copy-done.6
  25.9 0.6 broadcast_in_dim.135
  26.5 0.1 fusion.3
  26.6 0.0 copy-done.2
  26.6 0.8 convert_element_type.31.keep_ref
  27.4 0.0 copy-done.5
  27.4 0.1 copy.30
  27.5 0.1 reshape.117
  27.6 0.1 fusion.9
  27.7 0.6 gather_fusion.1
  28.3 0.1 pad.5.fresh_ref
  28.4 0.0 copy-done.4
  28.4 0.1 copy.34
  28.5 0.6 gather_fusion
  29.1 0.0 copy-done.1
  29.1 0.0 copy-start
  29.1 4.0 %copy-done = bf16[640,16,2,256]{3,2,1,0:T(2,128)(2,1)S(1)} copy-done((bf16[640,16,2,256]{3,2,1,0:T(2,128)(2,1)S(1)}, bf16[640,16,2,256]{3,2,1,0:T(2,128)(2,1)}, u32[]{:S(2)}) %copy-start) | copy-done | bytes 10485784
  33.1 30.8 %shard_map.106 = bf16[64,32,128]{2,1,0:T(8,128)(2,1)S(1)} custom-call(s32[640]{0:T(1024)S(1)} %copy-done.1, s32[64]{0:T(128)S(1)} %copy-done.2, bf16[64,32,128]{2,1,0:T(8,128)(2,1)S(1)} %bitcast.22, bf16[64,16,256]{2,1,0:T(8,128)(2,1)S(1)} %pad.5.fresh_ref, bf16[640,16,2,256]{3,2,1,0:T(2,128)(2,1)S(1)} %copy-done), custom_call_target="tpu_custom_call" | custom-call | flops 352321536 | bytes 20971520 | tf_op jit(solution)/shard_map/pallas_call | solution.py:77
  63.8 0.6 fusion.10
  64.4 0.6 iota_compare_fusion.4
  65.1 0.6 iota_compare_fusion.3
  65.7 0.0 all-gather.2.cloned.1.call-done
  65.8 1.0 convert_reduce_fusion
  66.7 0.2 fusion.6.count_ref
  66.9 2.9 %copy.31.pool_ref = bf16[88,16,2,256]{3,2,1,0:T(2,128)(2,1)S(1)} copy(bf16[88,16,2,256]{3,1,2,0:T(8,128)(2,1)} %all-gather.2.cloned.1.call-done) | data formatting | bytes 2883584 | tf_op jit(solution)/shard_map/all_gather | solution.py:332
  69.8 2.5 %shard_map.105 = bf16[2,32,128]{2,1,0:T(8,128)(2,1)S(1)} custom-call(s32[20]{0:T(128)S(1)} %add.34.table_ref, s32[2]{0:T(128)S(1)} %fusion.6.count_ref, bf16[2,32,128]{2,1,0:T(8,128)(2,1)S(1)} %gather_fusion, bf16[2,16,256]{2,1,0:T(8,128)(2,1)S(1)} %gather.11.fresh_ref, bf16[88,16,2,256]{3,2,1,0:T(2,128)(2,1)S(1)} %copy.31.pool_ref), custom_call_target="tpu_custom_call" | custom-call | flops 11010048 | bytes 2883584 | tf_op jit(solution)/shard_map/pallas_call | solution.py:77
  72.4 0.2 select_select_fusion
  72.6 0.1 reshape.118
  72.7 1.0 copy.32
  73.7 36.1 %shard_map.107 = (bf16[128,8192]{1,0:T(8,128)(2,1)}, bf16[128,8192]{1,0:T(8,128)(2,1)}) custom-call(bf16[128,2048]{1,0:T(8,128)(2,1)} %bitcast.23, f32[128,1]{1,0:T(8,128)} %convert_element_type.31.keep_ref, f32[1,8192]{1,0:T(1,128)} %bitcast.29, bf16[128,8192]{1,0:T(8,128)(2,1)} %bitcast.24, bf16[2048,8192]{1,0:T(8,128)(2,1)} %w_ref.1), custom_call_target="tpu_custom_call" | custom-call | flops 4294967296 | bytes 33554432 | tf_op jit(solution)/shard_map/pallas_call | solution.py:286
  109.8 0.0 copy-start.3
  109.8 3.2 %copy.37 = bf16[2,64,8192]{2,1,0:T(8,128)(2,1)} copy(bf16[2,64,8192]{2,1,0:T(8,128)(2,1)} %bitcast.26) | data formatting | bytes 4194304
  113.1 1.3 %copy.38 = bf16[2,64,8192]{2,1,0:T(8,128)(2,1)} copy(bf16[2,64,8192]{2,1,0:T(8,128)(2,1)S(1)} %bitcast.25) | data formatting | bytes 4194304
  (17 shorter events, 0.1 us)
Async XLA Ops:
  7.2 58.6 %all-gather.2.cloned.1.call-start = ((), (), s32[]{:S(2)}) async-start(), calls=%async_computation | async-start | bytes 1802240 | tf_op jit(solution)/shard_map/all_gather | solution.py:332
  10.1 1.4 %copy-start.7 = (s32[2]{0:T(128)}, s32[2]{0:T(128)S(1)}, u32[]{:S(2)}) copy-start(s32[2]{0:T(128)S(1)} %fusion.7.chosen_ref) | copy-start | bytes 28
  11.6 14.3 %copy-start.6 = (bf16[8192]{0:T(1024)(128)(2,1)S(1)}, bf16[8192]{0:T(1024)(128)(2,1)}, u32[]{:S(2)}) copy-start(bf16[8192]{0:T(1024)(128)(2,1)} %param.17) | copy-start | bytes 49156
  11.6 15.0 %copy-start.2 = (s32[64]{0:T(128)S(1)}, s32[64]{0:T(128)}, u32[]{:S(2)}) copy-start(s32[64]{0:T(128)} %count_ref.1) | copy-start | bytes 772
  11.6 15.8 %copy-start.5 = (bf16[2,64,2,256]{3,2,1,0:T(2,128)(2,1)S(1)}, bf16[2,64,2,256]{3,2,1,0:T(2,128)(2,1)}, u32[]{:S(2)}) copy-start(bf16[2,64,2,256]{3,2,1,0:T(2,128)(2,1)} %param.10) | copy-start | bytes 393220
  23.7 4.7 %copy-start.4 = (bf16[2,64,2048]{2,1,0:T(8,128)(2,1)S(1)}, bf16[2,64,2048]{2,1,0:T(8,128)(2,1)}, u32[]{:S(2)}) copy-start(bf16[2,64,2048]{2,1,0:T(8,128)(2,1)} %param.9) | copy-start | bytes 1572868
  25.5 3.6 %copy-start.1 = (s32[640]{0:T(1024)S(1)}, s32[640]{0:T(1024)}, u32[]{:S(2)}) copy-start(s32[640]{0:T(1024)} %reshape.114.table_ref) | copy-start | bytes 7684
  29.1 4.0 %copy-start = (bf16[640,16,2,256]{3,2,1,0:T(2,128)(2,1)S(1)}, bf16[640,16,2,256]{3,2,1,0:T(2,128)(2,1)}, u32[]{:S(2)}) copy-start(bf16[640,16,2,256]{3,2,1,0:T(2,128)(2,1)} %pool_ref.3) | copy-start | bytes 31457284
  109.8 3.3 %copy-start.3 = (bf16[128,8192]{1,0:T(8,128)(2,1)S(1)}, bf16[128,8192]{1,0:T(8,128)(2,1)}, u32[]{:S(2)}) copy-start(bf16[128,8192]{1,0:T(8,128)(2,1)} %get-tuple-element.5) | copy-start | bytes 6291460
Sparse Core Ops, SparseCore 0:
  25.6 37.6 all-gather.1

commit v2 on v1

--- a/solution.py
+++ b/solution.py
@@ -10,25 +10,14 @@
 
 SEND = 2
 CHUNK = 512
+VMEM_ASK = 58 * 2**20
 MESH = pl.DeviceIdType.MESH
 VMEM = pl.BlockSpec(memory_space=pltpu.VMEM)
 ANY = pl.BlockSpec(memory_space=pl.ANY)
 SMEM = pl.BlockSpec(memory_space=pltpu.SMEM)
 
 
-def attend_kernel(dims, table_ref, count_ref, query_ref, fresh_ref, pool_ref, out_ref, keys, values, sems):
-    slots, blocks, steps, heads, copies, unroll = dims
-    head_dim = query_ref.shape[-1]
-    rows = steps * heads
-    block_rows = keys.shape[1] * copies
-    cached = blocks * block_rows
-    fresh_pad = fresh_ref.shape[1]
-    total = cached + fresh_pad
-    get_keys = pltpu.make_async_copy(pool_ref.at[..., pl.ds(0, head_dim)], keys, sems.at[0])
-    get_values = pltpu.make_async_copy(pool_ref.at[..., pl.ds(head_dim, head_dim)], values, sems.at[1])
-    get_keys.start()
-    get_values.start()
-    inv_root = 1.0 / math.sqrt(head_dim)
+def masks(rows, heads, copies, cached, total):
     row = lax.broadcasted_iota(jnp.int32, (rows, total), 0)
     col = lax.broadcasted_iota(jnp.int32, (rows, total), 1)
     step = row // heads
@@ -37,41 +26,66 @@
     fresh_step = (col - cached) // copies
     same_copy = (col % copies) == copy
     fresh_ok = is_fresh & same_copy & (fresh_step <= step)
-    old_limit = jnp.where(is_fresh | jnp.logical_not(same_copy), 1 << 20, col)
+    limit = jnp.where(is_fresh | jnp.logical_not(same_copy), 1 << 20, col)
+    return jnp.where(fresh_ok, -1, limit)
+
+
+def attend_group(queries, keys, values, bounds, limit):
+    inv_root = 1.0 / math.sqrt(queries[0].shape[-1])
+    scores = [
+        lax.dot_general(q, k, (((1,), (1,)), ((), ())), preferred_element_type=jnp.float32)
+        for q, k in zip(queries, keys)
+    ]
+    scores = [jnp.where(limit < c, x * inv_root, -jnp.inf) for x, c in zip(scores, bounds)]
+    powers = [jnp.exp(x - jnp.max(x, axis=-1, keepdims=True)) for x in scores]
+    weights = [(p * (1.0 / jnp.sum(p, axis=-1, keepdims=True))).astype(jnp.bfloat16) for p in powers]
+    return [
+        jnp.dot(w, v, preferred_element_type=jnp.float32).astype(jnp.bfloat16) for w, v in zip(weights, values)
+    ]
+
+
+def attend_kernel(dims, table_ref, count_ref, query_ref, fresh_ref, pool_ref, out_ref, keys, values, sems):
+    slots, blocks, steps, heads, copies, unroll = dims
+    head_dim = query_ref.shape[-1]
+    rows = steps * heads
+    block_rows = keys.shape[1] * copies
+    cached = blocks * block_rows
+    get_keys = pltpu.make_async_copy(pool_ref.at[..., pl.ds(0, head_dim)], keys, sems.at[0])
+    get_values = pltpu.make_async_copy(pool_ref.at[..., pl.ds(head_dim, head_dim)], values, sems.at[1])
+    get_keys.start()
+    get_values.start()
+    limit = masks(rows, heads, copies, cached, cached + fresh_ref.shape[1])
     get_keys.wait()
     get_values.wait()
 
-    def one(n):
-        kk = [keys[table_ref[n * blocks + b]].reshape(block_rows, head_dim) for b in range(blocks)]
-        vv = [values[table_ref[n * blocks + b]].reshape(block_rows, head_dim) for b in range(blocks)]
-        new = fresh_ref[n]
-        kk = jnp.concatenate(kk + [new[:, :head_dim]], axis=0)
-        vv = jnp.concatenate(vv + [new[:, head_dim:]], axis=0)
-        scores = lax.dot_general(
-            query_ref[n], kk, (((1,), (1,)), ((), ())), preferred_element_type=jnp.float32
-        ) * inv_root
-        ok = fresh_ok | (old_limit < count_ref[n] * copies)
-        scores = jnp.where(ok, scores, -jnp.inf)
-        top = jnp.max(scores, axis=-1, keepdims=True)
-        powers = jnp.exp(scores - top)
-        denominator = jnp.sum(powers, axis=-1, keepdims=True)
-        weights = (powers / denominator).astype(jnp.bfloat16)
-        out_ref[n] = jnp.dot(weights, vv, preferred_element_type=jnp.float32).astype(jnp.bfloat16)
+    def rows_of(store, new, n):
+        found = [store[table_ref[n * blocks + b]].reshape(block_rows, head_dim) for b in range(blocks)]
+        return jnp.concatenate(found + [new], axis=0)
 
     def body(i, carry):
-        for u in range(unroll):
-            one(i * unroll + u)
+        ids = [i * unroll + u for u in range(unroll)]
+        new = [fresh_ref[n] for n in ids]
+        got = attend_group(
+            [query_ref[n] for n in ids],
+            [rows_of(keys, f[:, :head_dim], n) for f, n in zip(new, ids)],
+            [rows_of(values, f[:, head_dim:], n) for f, n in zip(new, ids)],
+            [count_ref[n] * copies for n in ids],
+            limit,
+        )
+        for n, x in zip(ids, got):
+            out_ref[n] = x
         return carry
 
     lax.fori_loop(0, slots // unroll, body, 0)
 
 
-def attend(query_rows, fresh_rows, pool, table, count, steps, copies):
+def drop_single(pool):
+    return pool.reshape(pool.shape[0], pool.shape[1], pool.shape[3]) if pool.shape[2] == 1 else pool
+
+
+def attend(query_rows, fresh_rows, pool, table, count, steps, copies, unroll):
     slots, rows, head_dim = query_rows.shape
     blocks = table.shape[1]
-    if copies == 1:
-        pool = pool.reshape(pool.shape[0], pool.shape[1], pool.shape[3])
-    unroll = 4 if slots % 4 == 0 else 1
     dims = (slots, blocks, steps, rows // steps, copies, unroll)
     part = pool.shape[:-1] + (head_dim,)
     return pl.pallas_call(
@@ -84,51 +98,99 @@
             pltpu.VMEM(part, jnp.bfloat16),
             pltpu.SemaphoreType.DMA((2,)),
         ],
-        compiler_params=pltpu.CompilerParams(vmem_limit_bytes=40 * 2**20),
+        compiler_params=pltpu.CompilerParams(vmem_limit_bytes=VMEM_ASK),
         cost_estimate=pl.CostEstimate(
             flops=4 * slots * rows * 336 * head_dim, bytes_accessed=4 * pool.size, transcendentals=slots * rows * 336
         ),
     )(table.reshape(-1), count, query_rows, fresh_rows, pool)
 
 
-def pack_kernel(blocks, table_ref, chosen_ref, size_ref, pool_ref, out_ref, note, sems):
+def moved_kernel(dims, from_ref, slot_ref, query_ref, fresh_ref, got_ref, main_ref, out_ref):
+    blocks, steps, heads, copies = dims
+    head_dim = query_ref.shape[-1]
+    rows = steps * heads
+    cached = blocks * got_ref.shape[1]
+    limit = masks(rows, heads, copies, cached, cached + fresh_ref.shape[1])
+    out_ref[...] = main_ref[...]
+    ids = [jnp.maximum(slot_ref[j], 0) for j in range(SEND)]
+    base = [from_ref[j] * (blocks + 1) for j in range(SEND)]
+
+    def rows_of(j, lo):
+        found = [got_ref[base[j] + b, :, lo : lo + head_dim] for b in range(blocks)]
+        return jnp.concatenate(found + [fresh_ref[ids[j], :, lo : lo + head_dim]], axis=0)
+
+    bounds = [
+        got_ref[base[j] + blocks, :, 0:head_dim].astype(jnp.float32)[0:1, 0:1].astype(jnp.int32) * copies
+        for j in range(SEND)
+    ]
+    heads_of = attend_group(
+        [query_ref[n] for n in ids],
+        [rows_of(j, 0) for j in range(SEND)],
+        [rows_of(j, head_dim) for j in range(SEND)],
+        bounds,
+        limit,
+    )
+    for j in range(SEND):
+
+        @pl.when(slot_ref[j] >= 0)
+        def _():
+            out_ref[ids[j]] = heads_of[j]
+
+
+def attend_moved(query_rows, fresh_rows, got, from_index, to_slot, main, blocks, steps, copies):
+    rows = query_rows.shape[1]
+    dims = (blocks, steps, rows // steps, copies)
+    return pl.pallas_call(
+        functools.partial(moved_kernel, dims),
+        out_shape=jax.ShapeDtypeStruct(main.shape, main.dtype),
+        in_specs=[SMEM, SMEM, VMEM, VMEM, VMEM, VMEM],
+        out_specs=VMEM,
+    )(from_index, to_slot, query_rows, fresh_rows, got, main)
+
+
+def pack_kernel(blocks, head_dim, table_ref, chosen_ref, size_ref, pool_ref, out_ref, keys, values, sems):
     copies = []
     for j in range(SEND):
         for b in range(blocks):
-            copies.append(
-                pltpu.make_async_copy(
-                    pool_ref.at[table_ref[chosen_ref[j] * blocks + b]],
-                    out_ref.at[j * (blocks + 1) + b],
-                    sems.at[j * (blocks + 1) + b],
-                )
-            )
-            copies[-1].start()
+            at = j * blocks + b
+            block = pool_ref.at[table_ref[chosen_ref[j] * blocks + b]]
+            for half, store in enumerate((keys, values)):
+                part = block.at[..., pl.ds(half * head_dim, head_dim)]
+                copies.append(pltpu.make_async_copy(part, store.at[at], sems.at[2 * at + half]))
+                copies[-1].start()
+    shape = out_ref.shape[1:]
     for j in range(SEND):
-        size = jnp.full(note.shape[1:], size_ref[j], jnp.int32)
-        note[j] = size.astype(jnp.float32).astype(jnp.bfloat16)
-        at = j * (blocks + 1) + blocks
-        copies.append(pltpu.make_async_copy(note.at[j], out_ref.at[at], sems.at[at]))
-        copies[-1].start()
+        size = jnp.full(shape, size_ref[j], jnp.int32)
+        out_ref[j * (blocks + 1) + blocks] = size.astype(jnp.float32).astype(jnp.bfloat16)
     for copy in copies:
         copy.wait()
-
-
-def pack(pool, table, chosen, sizes):
+    for j in range(SEND):
+        for b in range(blocks):
+            for half, store in enumerate((keys, values)):
+                cols = pl.ds(half * head_dim, head_dim)
+                out_ref[j * (blocks + 1) + b, :, cols] = store[j * blocks + b].reshape(shape[0], head_dim)
+
+
+def pack(pool, table, chosen, sizes, copies):
     blocks = table.shape[1]
-    count = SEND * (blocks + 1)
+    head_dim = pool.shape[-1] // 2
+    part = pool.shape[1:-1] + (head_dim,)
+    shape = (SEND * (blocks + 1), pool.shape[1] * copies, 2 * head_dim)
     return pl.pallas_call(
-        functools.partial(pack_kernel, blocks),
-        out_shape=jax.ShapeDtypeStruct((count,) + pool.shape[1:], pool.dtype),
+        functools.partial(pack_kernel, blocks, head_dim),
+        out_shape=jax.ShapeDtypeStruct(shape, pool.dtype),
         in_specs=[SMEM, SMEM, SMEM, ANY],
-        out_specs=ANY,
+        out_specs=VMEM,
         scratch_shapes=[
-            pltpu.VMEM((SEND,) + pool.shape[1:], pool.dtype),
-            pltpu.SemaphoreType.DMA((count,)),
+            pltpu.VMEM((SEND * blocks,) + part, pool.dtype),
+            pltpu.VMEM((SEND * blocks,) + part, pool.dtype),
+            pltpu.SemaphoreType.DMA((2 * SEND * blocks,)),
         ],
+        compiler_params=pltpu.CompilerParams(vmem_limit_bytes=VMEM_ASK),
     )(table.reshape(-1), chosen, sizes, pool)
 
 
-def project_kernel(ranks, head_ref, keep_ref, gain_ref, resid_ref, w_ref, hidden_ref, normed_ref,
+def project_kernel(ranks, head_ref, keep_ref, resid_ref, w_ref, hidden_ref, scale_ref,
                    weight, sib_out, sib_in, y_out, y_in, whole, w_sem, s_send, s_recv, y_send, y_recv,
                    g_send, g_recv, h_send, h_recv):
     rows, width = hidden_ref.shape
@@ -257,12 +319,9 @@
             slot, copy = hand_over(sib_side, off, k)
             copy.wait_recv()
             squares = squares + square(slot)
-    scale = lax.rsqrt(squares * (1.0 / width) + 1e-05)
+    scale_ref[...] = lax.rsqrt(squares * (1.0 / width) + 1e-05)
     for j in range(width // CHUNK):
-        cols = pl.ds(j * CHUNK, CHUNK)
-        hidden = whole[j]
-        hidden_ref[:, cols] = hidden
-        normed_ref[:, cols] = (hidden.astype(jnp.float32) * scale * gain_ref[:, cols]).astype(jnp.bfloat16)
+        hidden_ref[:, pl.ds(j * CHUNK, CHUNK)] = whole[j]
     for i in range(steps):
         to_sibling(i).wait_send()
     for i in range(steps - pieces):
@@ -274,7 +333,7 @@
             hand_over(core, off, k)[1].wait_send()
 
 
-def project(flat_heads, keep_rows, gain, resid_rows, w_out, ranks):
+def project(flat_heads, keep_rows, resid_rows, w_out, ranks):
     rows = flat_heads.shape[0]
     depth, width = w_out.shape
     pieces = width // ranks // CHUNK
@@ -285,8 +344,8 @@
     out = jax.ShapeDtypeStruct((rows, width), jnp.bfloat16)
     return pl.pallas_call(
         functools.partial(project_kernel, ranks),
-        out_shape=(out, out),
-        in_specs=[VMEM, VMEM, VMEM, VMEM, ANY],
+        out_shape=(out, jax.ShapeDtypeStruct((rows, 1), jnp.float32)),
+        in_specs=[VMEM, VMEM, VMEM, ANY],
         out_specs=(VMEM, VMEM),
         scratch_shapes=[
             pltpu.VMEM((2 * steps, depth, CHUNK), jnp.bfloat16),
@@ -307,7 +366,7 @@
         cost_estimate=pl.CostEstimate(
             flops=2 * rows * depth * width, bytes_accessed=2 * depth * width, transcendentals=0
         ),
-    )(flat_heads, keep_rows, gain, resid_rows, w_out)
+    )(flat_heads, keep_rows, resid_rows, w_out)
 
 
 def per_device(ranks, queries, new_kv, pool, lengths, block_table, plan, w_out, residual, norm_gain):
@@ -329,28 +388,21 @@
     selector = sending[None, :] & (position[None, :] == ranks_of[:, None])
     chosen = jnp.sum(jnp.where(selector, source_slot[None, :], 0), axis=1)
     sizes = jnp.sum(jnp.where(slot_ids[None, :] == chosen[:, None], lengths[None, :], 0), axis=1)
-    got = lax.all_gather(pack(pool, block_table, chosen, sizes), "replica", axis=0, tiled=True)
+    pool = drop_single(pool)
+    got = lax.all_gather(pack(pool, block_table, chosen, sizes, copies), "replica", axis=0, tiled=True)
 
     query_rows = queries.reshape(steps, slots, heads, head_dim).transpose(1, 0, 2, 3)
     query_rows = query_rows.reshape(slots, steps * heads, head_dim)
     fresh_rows = new_kv.transpose(1, 0, 2, 3).reshape(slots, steps * copies, 2 * head_dim)
     fresh_rows = jnp.pad(fresh_rows, ((0, 0), (0, 16 - steps * copies), (0, 0)))
-    main = attend(query_rows, fresh_rows, pool, block_table, lengths, steps, copies)
+    main = attend(query_rows, fresh_rows, pool, block_table, lengths, steps, copies, 8)
 
     turn = jnp.sum((target[None, :] == target[:, None]) & before, axis=1)
     arrival = arriving[None, :] & (turn[None, :] == ranks_of[:, None])
     from_index = jnp.sum(jnp.where(arrival, (source * SEND + position)[None, :], 0), axis=1)
     to_slot = jnp.sum(jnp.where(arrival, target_slot[None, :], 0), axis=1)
     to_slot = jnp.where(jnp.any(arrival, axis=1), to_slot, -1)
-    got_sizes = got[blocks :: blocks + 1, 0, 0, 0].astype(jnp.int32)
-    moved_hit = jnp.arange(got_sizes.shape[0], dtype=jnp.int32)[None, :] == from_index[:, None]
-    moved_count = jnp.sum(jnp.where(moved_hit, got_sizes[None, :], 0), axis=1)
-    moved_table = from_index[:, None] * (blocks + 1) + jnp.arange(blocks, dtype=jnp.int32)[None, :]
-    pick = jnp.maximum(to_slot, 0)
-    extra = attend(query_rows[pick], fresh_rows[pick], got, moved_table, moved_count, steps, copies)
-    head_out = main
-    for j in range(SEND):
-        head_out = jnp.where((slot_ids == to_slot[j])[:, None, None], extra[j][None], head_out)
+    head_out = attend_moved(query_rows, fresh_rows, got, from_index, to_slot, main, blocks, steps, copies)
     flat_heads = head_out.reshape(slots, steps, heads * head_dim).transpose(1, 0, 2)
     flat_heads = flat_heads.reshape(steps * slots, heads * head_dim)
 
@@ -358,9 +410,10 @@
     moved_out = jnp.any(sending[None, :] & (source_slot[None, :] == slot_ids[:, None]), axis=1)
     live = incoming | (lengths > 0) & jnp.logical_not(moved_out)
     keep_rows = jnp.tile(live, steps)[:, None].astype(jnp.float32)
+    resid_rows = residual.reshape(steps * slots, width)
+    hidden, scale = project(flat_heads, keep_rows, resid_rows, w_out, ranks)
     gain = norm_gain.astype(jnp.float32)[None, :]
-    resid_rows = residual.reshape(steps * slots, width)
-    hidden, normed = project(flat_heads, keep_rows, gain, resid_rows, w_out, ranks)
+    normed = (hidden.astype(jnp.float32) * scale * gain).astype(jnp.bfloat16)
     out_shape = (steps, slots, width)
     return (hidden.reshape(out_shape), normed.reshape(out_shape))
 

time: 122 us -> 104 us (0.85)
  Pallas kernels: 81.5 us -> 52.2 us
  waiting for transfers between devices: 0.04 us -> 21.1 us
  local copies, waits for them, and re-layouts: 19.9 us -> 8.74 us
  other arithmetic: 5.48 us -> 7.86 us
    all_gather x1, waiting for transfers between devices: 0.02 us -> 21.1 us  [per_device(): lax.all_gather(pack(pool, block_table, chosen, sizes, copies), 'replica',...]
    pallas_call x2 -> x1, Pallas kernels: 33.3 us -> 12.7 us  [attend(): pl.pallas_call(functools.partial(attend_kernel, dims), out_shape=jax.Shap...]
    unnamed x20 -> x15, local copies, waits for them, and re-layouts: 9.47 us -> 2.24 us
    pallas_call x1 -> x2, Pallas kernels: 12.1 us -> 6.21 us  [the longest x1 3.11 us: attend_moved(): pl.pallas_call(functools.partial(moved_kernel, dims), out_shape=jax.Shape...]
    all_gather x1 -> x0, local copies, waits for them, and re-layouts: 2.94 us -> none  [per_device(): lax.all_gather(pack(pool, block_table, chosen, sizes), 'replica', axis=0,...]
    pallas_call x1, Pallas kernels: 36.1 us -> 33.3 us  [project(): pl.pallas_call(functools.partial(project_kernel, ranks), out_shape=(out,...]
    convert_element_type x1 -> x2, other arithmetic: 0.96 us -> 3.5 us  [the longest x1 3.5 us: per_device(): normed = (hidden.astype(jnp.float32) * scale * gain).astype(jnp.bfloat16)]
    pallas_call x1 -> x0, local copies, waits for them, and re-layouts: 1.83 us -> none  [pack(): pl.pallas_call(functools.partial(pack_kernel, blocks), out_shape=jax.Shap...]
  transfers between devices with their start and end apart: 1 -> 1, of which waited for: 0 -> 1; matrix products, arithmetic and copies ran while one was open for 4% -> 4% of each run, Pallas kernels for 25% -> 12%
where the time goes in v2:
time: 104 us
  Pallas kernels  52.2 us (50%)
  waiting for transfers between devices  21.1 us (20%)
  between operations  14.2 us (14%)
  local copies, waits for them, and re-layouts  8.74 us (8%)
  other arithmetic  7.86 us (8%)
    pallas_call x1, Pallas kernels, project(): pl.pallas_call(functools.partial(project_kernel, ranks), out_shape=(out,...  33.3 us
    all_gather x1, waiting for transfers between devices, per_device(): lax.all_gather(pack(pool, block_table, chosen, sizes, copies), 'replica',...  21.1 us
    pallas_call x1, Pallas kernels, attend(): pl.pallas_call(functools.partial(attend_kernel, dims), out_shape=jax.Shap...  12.7 us
    convert_element_type x1, other arithmetic, per_device(): normed = (hidden.astype(jnp.float32) * scale * gain).astype(jnp.bfloat16)  3.5 us
    pallas_call x1, Pallas kernels, attend_moved(): pl.pallas_call(functools.partial(moved_kernel, dims), out_shape=jax.Shape...  3.11 us
    pallas_call x1, Pallas kernels, pack(): pl.pallas_call(functools.partial(pack_kernel, blocks, head_dim), out_shap...  3.1 us
    unnamed x15, local copies, waits for them, and re-layouts  2.24 us
    reshape x2, local copies, waits for them, and re-layouts, per_device(): head_out.reshape(slots, steps, heads * head_dim).transpose(1, 0, 2)  2.12 us
  transfers between devices with their start and end apart: 1, of which 1 were waited for; matrix products, arithmetic and copies ran while one was open for 4% of the time, Pallas kernels for 12%

profile of v2, /device:TPU:0, one launch (start us, length us, event | category | flops | bytes accessed | tf_op | source)
XLA Modules:
  0.0 104.1 jit_solution(9061980342808856948)
XLA Ops:
  7.2 0.0 all-gather.2.cloned.1.call-start
  7.2 1.0 %slice_reduce_fusion = (s32[4]{0:T(128)S(1)}, s32[4]{0:T(128)S(1)}, s32[4]{0:T(128)S(1)}, s32[4]{0:T(128)S(1)}) fusion(s32[4,4]{1,0:T(4,128)} %param.14), kind=kLoop, calls=%fused_computation.3 | loop fusion | bytes 128 | tf_op jit(solution)/shard_map/slice | solution.py:380
  8.3 0.2 convert_reduce_fusion
  8.5 0.8 copy.27
  9.2 0.7 reshape.76.table_ref
  10.0 0.1 fusion.6.chosen_ref
  10.1 0.0 copy-start.5
  10.1 1.3 %fusion.7.size_ref = s32[2]{0:T(128)} fusion(s32[64]{0:T(128)} %count_ref.1, s32[2]{0:T(128)S(1)} %fusion.6.chosen_ref), kind=kLoop, calls=%fused_computation.21 | loop fusion | flops 382 | bytes 272 | tf_op jit(solution)/shard_map/reduce_sum | solution.py:390
  11.4 0.0 copy-done.5
  11.4 0.0 copy-start.3
  11.5 0.0 copy-start.4
  11.5 0.0 copy-start.2
  11.5 0.0 copy-start.1
  11.5 3.1 %shard_map.104 = bf16[22,32,256]{2,1,0:T(8,128)(2,1)} custom-call(s32[640]{0:T(1024)} %reshape.76.table_ref, s32[2]{0:T(128)} %copy-done.5, s32[2]{0:T(128)} %fusion.7.size_ref, bf16[640,16,2,256]{3,2,1,0:T(2,128)(2,1)} %pool_ref.3), custom_call_target="tpu_custom_call" | custom-call | tf_op jit(solution)/shard_map/pallas_call | solution.py:179
  14.6 0.0 all-gather.2.cloned.1.call-update
  14.6 0.0 copy-done.3
  14.6 0.1 fusion.3
  14.7 0.0 copy-done.4
  14.8 0.8 convert_element_type.29.keep_ref
  15.5 0.0 copy-done.2
  15.5 0.1 copy.26
  15.6 0.1 reshape.75
  15.7 0.0 copy-done.1
  15.7 0.1 copy.30
  15.8 0.8 copy.25
  16.7 0.8 pad.4.fresh_ref
  17.5 12.7 %shard_map.105.main_ref = bf16[64,32,128]{2,1,0:T(8,128)(2,1)} custom-call(s32[640]{0:T(1024)} %reshape.76.table_ref, s32[64]{0:T(128)} %count_ref.1, bf16[64,32,128]{2,1,0:T(8,128)(2,1)} %bitcast.15, bf16[64,16,256]{2,1,0:T(8,128)(2,1)} %pad.4.fresh_ref, bf16[640,16,2,256]{3,2,1,0:T(2,128)(2,1)} %pool_ref.3), custom_call_target="tpu_custom_call" | custom-call | flops 352321536 | bytes 20971520 | tf_op jit(solution)/shard_map/pallas_call | solution.py:91
  30.2 0.2 convert_reduce_fusion.1
  30.4 0.1 fusion.8
  30.5 0.7 select_reduce_fusion
  31.2 0.5 broadcast_select_fusion.slot_ref
  31.7 21.1 %all-gather.2.cloned.1.call-done.got_ref = bf16[88,32,256]{2,1,0:T(8,128)(2,1)} async-done(((bf16[22,32,256]{2,1,0:T(8,128)(2,1)}), bf16[88,32,256]{2,1,0:T(8,128)(2,1)}) %all-gather.2.cloned.1.call-update) | async-done | bytes 1441808 | tf_op jit(solution)/shard_map/all_gather | solution.py:392
  52.8 3.1 %shard_map.106 = bf16[64,32,128]{2,1,0:T(8,128)(2,1)} custom-call(s32[2]{0:T(128)} %get-tuple-element.11.from_ref, s32[2]{0:T(128)} %broadcast_select_fusion.slot_ref, bf16[64,32,128]{2,1,0:T(8,128)(2,1)} %bitcast.16, bf16[64,16,256]{2,1,0:T(8,128)(2,1)} %pad.4.fresh_ref, bf16[88,32,256]{2,1,0:T(8,128)(2,1)} %all-gather.2.cloned.1.call-done.got_ref, ...), custom_call_target="tpu_custom_call" | custom-call | tf_op jit(solution)/shard_map/pallas_call | solution.py:143
  55.9 1.2 %reshape.77 = bf16[64,2,2048]{2,1,0:T(2,128)(2,1)S(1)} reshape(bf16[64,32,128]{2,1,0:T(8,128)(2,1)} %shard_map.106) | data formatting | bytes 1048576 | tf_op jit(solution)/shard_map/reshape | solution.py:406
  57.1 1.0 copy.28
  58.0 33.3 %shard_map.107 = (bf16[128,8192]{1,0:T(8,128)(2,1)}, f32[128,1]{1,0:T(8,128)}) custom-call(bf16[128,2048]{1,0:T(8,128)(2,1)} %bitcast.17, f32[128,1]{1,0:T(8,128)} %convert_element_type.29.keep_ref, bf16[128,8192]{1,0:T(8,128)(2,1)} %bitcast.18, bf16[2048,8192]{1,0:T(8,128)(2,1)} %w_ref.1), custom_call_target="tpu_custom_call" | custom-call | flops 4294967296 | bytes 33554432 | tf_op jit(solution)/shard_map/pallas_call | solution.py:345
  91.3 0.0 copy-start
  91.3 1.1 %reduce.4 = f32[128]{0:T(128)S(1)} reduce(f32[128,1]{1,0:T(8,128)} %get-tuple-element.5, f32[]{:T(128)} %constant.24), dimensions={1}, to_apply=%get-tuple-element.5.reduce_sub_computation | reduce | bytes 1028 | tf_op jit(solution)/shard_map/pallas_call | solution.py:345
  92.4 3.5 %multiply_convert_fusion = bf16[128,8192]{1,0:T(8,128)(2,1)} fusion(bf16[128,8192]{1,0:T(8,128)(2,1)} %get-tuple-element.4, f32[8192]{0:T(1024)S(1)} %convert_element_type.27, f32[128]{0:T(128)S(1)} %reduce.4), kind=kLoop, calls=%fused_computation | loop fusion | flops 4194304 | bytes 4227584 | tf_op jit(solution)/shard_map/convert_element_type | solution.py:416
  95.9 0.0 copy-done
  95.9 1.3 %copy.32 = bf16[2,64,8192]{2,1,0:T(8,128)(2,1)} copy(bf16[2,64,8192]{2,1,0:T(8,128)(2,1)S(1)} %bitcast.14) | data formatting | bytes 4194304
  (6 shorter events, 0.0 us)
Async XLA Ops:
  7.2 45.6 %all-gather.2.cloned.1.call-start = ((), (), s32[]{:S(2)}) async-start(), calls=%async_computation | async-start | bytes 1802240 | tf_op jit(solution)/shard_map/all_gather | solution.py:392
  10.1 1.4 %copy-start.5 = (s32[2]{0:T(128)}, s32[2]{0:T(128)S(1)}, u32[]{:S(2)}) copy-start(s32[2]{0:T(128)S(1)} %fusion.6.chosen_ref) | copy-start | bytes 28
  11.4 3.2 %copy-start.3 = (bf16[8192]{0:T(1024)(128)(2,1)S(1)}, bf16[8192]{0:T(1024)(128)(2,1)}, u32[]{:S(2)}) copy-start(bf16[8192]{0:T(1024)(128)(2,1)} %param.17) | copy-start | bytes 49156
  11.5 3.3 %copy-start.4 = (s32[64]{0:T(128)S(1)}, s32[64]{0:T(128)}, u32[]{:S(2)}) copy-start(s32[64]{0:T(128)} %count_ref.1) | copy-start | bytes 772
  11.5 4.1 %copy-start.2 = (bf16[2,64,2,256]{3,2,1,0:T(2,128)(2,1)S(1)}, bf16[2,64,2,256]{3,2,1,0:T(2,128)(2,1)}, u32[]{:S(2)}) copy-start(bf16[2,64,2,256]{3,2,1,0:T(2,128)(2,1)} %param.10) | copy-start | bytes 393220
  11.5 4.2 %copy-start.1 = (bf16[2,64,2048]{2,1,0:T(8,128)(2,1)S(1)}, bf16[2,64,2048]{2,1,0:T(8,128)(2,1)}, u32[]{:S(2)}) copy-start(bf16[2,64,2048]{2,1,0:T(8,128)(2,1)} %param.9) | copy-start | bytes 1572868
  91.3 4.6 %copy-start = (bf16[128,8192]{1,0:T(8,128)(2,1)S(1)}, bf16[128,8192]{1,0:T(8,128)(2,1)}, u32[]{:S(2)}) copy-start(bf16[128,8192]{1,0:T(8,128)(2,1)} %get-tuple-element.4) | copy-start | bytes 6291460
Sparse Core Ops, SparseCore 0:
  14.7 38.0 all-gather.1

commit v3 on v2

--- a/solution.py
+++ b/solution.py
@@ -8,7 +8,6 @@
 from jax.experimental.pallas import tpu as pltpu
 from jax.sharding import PartitionSpec as P
 
-SEND = 2
 CHUNK = 512
 VMEM_ASK = 58 * 2**20
 MESH = pl.DeviceIdType.MESH
@@ -105,52 +104,54 @@
     )(table.reshape(-1), count, query_rows, fresh_rows, pool)
 
 
-def moved_kernel(dims, from_ref, slot_ref, query_ref, fresh_ref, got_ref, main_ref, out_ref):
+def moved_kernel(dims, slot_ref, query_ref, fresh_ref, main_ref, *refs):
     blocks, steps, heads, copies = dims
+    got_refs, out_ref = refs[:-1], refs[-1]
+    moves = range(len(got_refs))
     head_dim = query_ref.shape[-1]
     rows = steps * heads
-    cached = blocks * got_ref.shape[1]
+    cached = blocks * got_refs[0].shape[1]
     limit = masks(rows, heads, copies, cached, cached + fresh_ref.shape[1])
     out_ref[...] = main_ref[...]
-    ids = [jnp.maximum(slot_ref[j], 0) for j in range(SEND)]
-    base = [from_ref[j] * (blocks + 1) for j in range(SEND)]
+    ids = [jnp.maximum(slot_ref[j], 0) for j in moves]
 
     def rows_of(j, lo):
-        found = [got_ref[base[j] + b, :, lo : lo + head_dim] for b in range(blocks)]
+        found = [got_refs[j][b, :, lo : lo + head_dim] for b in range(blocks)]
         return jnp.concatenate(found + [fresh_ref[ids[j], :, lo : lo + head_dim]], axis=0)
 
     bounds = [
-        got_ref[base[j] + blocks, :, 0:head_dim].astype(jnp.float32)[0:1, 0:1].astype(jnp.int32) * copies
-        for j in range(SEND)
+        got_refs[j][blocks, :, 0:head_dim].astype(jnp.float32)[0:1, 0:1].astype(jnp.int32) * copies
+        for j in moves
     ]
     heads_of = attend_group(
         [query_ref[n] for n in ids],
-        [rows_of(j, 0) for j in range(SEND)],
-        [rows_of(j, head_dim) for j in range(SEND)],
+        [rows_of(j, 0) for j in moves],
+        [rows_of(j, head_dim) for j in moves],
         bounds,
         limit,
     )
-    for j in range(SEND):
+    for j in moves:
 
         @pl.when(slot_ref[j] >= 0)
         def _():
             out_ref[ids[j]] = heads_of[j]
 
 
-def attend_moved(query_rows, fresh_rows, got, from_index, to_slot, main, blocks, steps, copies):
+def attend_moved(query_rows, fresh_rows, got, to_slot, main, blocks, steps, copies):
     rows = query_rows.shape[1]
     dims = (blocks, steps, rows // steps, copies)
     return pl.pallas_call(
         functools.partial(moved_kernel, dims),
         out_shape=jax.ShapeDtypeStruct(main.shape, main.dtype),
-        in_specs=[SMEM, SMEM, VMEM, VMEM, VMEM, VMEM],
+        in_specs=[SMEM, VMEM, VMEM, VMEM] + [VMEM] * len(got),
         out_specs=VMEM,
-    )(from_index, to_slot, query_rows, fresh_rows, got, main)
-
-
-def pack_kernel(blocks, head_dim, table_ref, chosen_ref, size_ref, pool_ref, out_ref, keys, values, sems):
+    )(to_slot, query_rows, fresh_rows, main, *got)
+
+
+def pack_kernel(blocks, head_dim, table_ref, chosen_ref, size_ref, pool_ref, *refs):
+    out_refs, (keys, values, sems) = refs[:-3], refs[-3:]
     copies = []
-    for j in range(SEND):
+    for j in range(len(out_refs)):
         for b in range(blocks):
             at = j * blocks + b
             block = pool_ref.at[table_ref[chosen_ref[j] * blocks + b]]
@@ -158,33 +159,34 @@
                 part = block.at[..., pl.ds(half * head_dim, head_dim)]
                 copies.append(pltpu.make_async_copy(part, store.at[at], sems.at[2 * at + half]))
                 copies[-1].start()
-    shape = out_ref.shape[1:]
-    for j in range(SEND):
+    shape = out_refs[0].shape[1:]
+    for j, out_ref in enumerate(out_refs):
         size = jnp.full(shape, size_ref[j], jnp.int32)
-        out_ref[j * (blocks + 1) + blocks] = size.astype(jnp.float32).astype(jnp.bfloat16)
+        out_ref[blocks] = size.astype(jnp.float32).astype(jnp.bfloat16)
     for copy in copies:
         copy.wait()
-    for j in range(SEND):
+    for j, out_ref in enumerate(out_refs):
         for b in range(blocks):
             for half, store in enumerate((keys, values)):
                 cols = pl.ds(half * head_dim, head_dim)
-                out_ref[j * (blocks + 1) + b, :, cols] = store[j * blocks + b].reshape(shape[0], head_dim)
+                out_ref[b, :, cols] = store[j * blocks + b].reshape(shape[0], head_dim)
 
 
 def pack(pool, table, chosen, sizes, copies):
     blocks = table.shape[1]
+    moves = chosen.shape[0]
     head_dim = pool.shape[-1] // 2
-    part = pool.shape[1:-1] + (head_dim,)
-    shape = (SEND * (blocks + 1), pool.shape[1] * copies, 2 * head_dim)
+    part = (moves * blocks,) + pool.shape[1:-1] + (head_dim,)
+    out = jax.ShapeDtypeStruct((blocks + 1, pool.shape[1] * copies, 2 * head_dim), pool.dtype)
     return pl.pallas_call(
         functools.partial(pack_kernel, blocks, head_dim),
-        out_shape=jax.ShapeDtypeStruct(shape, pool.dtype),
+        out_shape=(out,) * moves,
         in_specs=[SMEM, SMEM, SMEM, ANY],
-        out_specs=VMEM,
+        out_specs=(VMEM,) * moves,
         scratch_shapes=[
-            pltpu.VMEM((SEND * blocks,) + part, pool.dtype),
-            pltpu.VMEM((SEND * blocks,) + part, pool.dtype),
-            pltpu.SemaphoreType.DMA((2 * SEND * blocks,)),
+            pltpu.VMEM(part, pool.dtype),
+            pltpu.VMEM(part, pool.dtype),
+            pltpu.SemaphoreType.DMA((2 * moves * blocks,)),
         ],
         compiler_params=pltpu.CompilerParams(vmem_limit_bytes=VMEM_ASK),
     )(table.reshape(-1), chosen, sizes, pool)
@@ -369,7 +371,7 @@
     )(flat_heads, keep_rows, resid_rows, w_out)
 
 
-def per_device(ranks, queries, new_kv, pool, lengths, block_table, plan, w_out, residual, norm_gain):
+def per_device(replicas, ranks, queries, new_kv, pool, lengths, block_table, plan, w_out, residual, norm_gain):
     my_replica = lax.axis_index("replica")
     steps, slots, _ = queries.shape
     head_dim = pool.shape[3] // 2
@@ -378,18 +380,18 @@
     blocks = block_table.shape[1]
     width = w_out.shape[1]
     source_slot, source, target, target_slot = (plan[:, i] for i in range(4))
-    order = jnp.arange(plan.shape[0], dtype=jnp.int32)
     slot_ids = jnp.arange(slots, dtype=jnp.int32)
-    ranks_of = jnp.arange(SEND, dtype=jnp.int32)
     sending = source == my_replica
     arriving = target == my_replica
-    before = order[None, :] < order[:, None]
-    position = jnp.sum((source[None, :] == source[:, None]) & before, axis=1)
-    selector = sending[None, :] & (position[None, :] == ranks_of[:, None])
-    chosen = jnp.sum(jnp.where(selector, source_slot[None, :], 0), axis=1)
+    shifts = jnp.arange(1, replicas, dtype=jnp.int32)
+    leaving = sending[None, :] & (target[None, :] == ((my_replica + shifts) % replicas)[:, None])
+    chosen = jnp.sum(jnp.where(leaving, source_slot[None, :], 0), axis=1)
     sizes = jnp.sum(jnp.where(slot_ids[None, :] == chosen[:, None], lengths[None, :], 0), axis=1)
     pool = drop_single(pool)
-    got = lax.all_gather(pack(pool, block_table, chosen, sizes, copies), "replica", axis=0, tiled=True)
+    got = [
+        lax.ppermute(block, "replica", [(r, (r + d) % replicas) for r in range(replicas)])
+        for d, block in enumerate(pack(pool, block_table, chosen, sizes, copies), 1)
+    ]
 
     query_rows = queries.reshape(steps, slots, heads, head_dim).transpose(1, 0, 2, 3)
     query_rows = query_rows.reshape(slots, steps * heads, head_dim)
@@ -397,12 +399,9 @@
     fresh_rows = jnp.pad(fresh_rows, ((0, 0), (0, 16 - steps * copies), (0, 0)))
     main = attend(query_rows, fresh_rows, pool, block_table, lengths, steps, copies, 8)
 
-    turn = jnp.sum((target[None, :] == target[:, None]) & before, axis=1)
-    arrival = arriving[None, :] & (turn[None, :] == ranks_of[:, None])
-    from_index = jnp.sum(jnp.where(arrival, (source * SEND + position)[None, :], 0), axis=1)
-    to_slot = jnp.sum(jnp.where(arrival, target_slot[None, :], 0), axis=1)
-    to_slot = jnp.where(jnp.any(arrival, axis=1), to_slot, -1)
-    head_out = attend_moved(query_rows, fresh_rows, got, from_index, to_slot, main, blocks, steps, copies)
+    arrival = arriving[None, :] & (source[None, :] == ((my_replica - shifts) % replicas)[:, None])
+    to_slot = jnp.sum(jnp.where(arrival, target_slot[None, :] + 1, 0), axis=1) - 1
+    head_out = attend_moved(query_rows, fresh_rows, got, to_slot, main, blocks, steps, copies)
     flat_heads = head_out.reshape(slots, steps, heads * head_dim).transpose(1, 0, 2)
     flat_heads = flat_heads.reshape(steps * slots, heads * head_dim)
 
@@ -432,6 +431,6 @@
     )
     out_specs = (P(None, ("groups", "replica"), None), P(None, ("groups", "replica"), None))
     return jax.shard_map(
-        functools.partial(per_device, mesh.shape["tensor"]),
+        functools.partial(per_device, mesh.shape["replica"], mesh.shape["tensor"]),
         mesh=mesh, in_specs=in_specs, out_specs=out_specs, check_vma=False,
     )

time: 104 us -> 77.8 us (0.75)
  waiting for transfers between devices: 21.1 us -> 0.01 us
  between operations: 14.2 us -> 0.79 us
  starting transfers between devices: 0.04 us -> 6.55 us
  local copies, waits for them, and re-layouts: 8.74 us -> 10.1 us
    all_gather x1 -> x0, waiting for transfers between devices: 21.1 us -> none  [per_device(): lax.all_gather(pack(pool, block_table, chosen, sizes, copies), 'replica',...]
    ppermute x0 -> x3, starting transfers between devices: none -> 6.55 us  [per_device(): lax.ppermute(block, 'replica', [(r, (r + d) % replicas) for r in range(re...]
    unnamed x15 -> x21, local copies, waits for them, and re-layouts: 2.24 us -> 3.64 us
  transfers between devices with their start and end apart: 1 -> 3, of which waited for: 1 -> 0; matrix products, arithmetic and copies ran while one was open for 4% -> 5% of each run, Pallas kernels for 12% -> 16%
where the time goes in v3:
time: 77.8 us; the launch traced here: 77.3 us
  Pallas kernels  52.8 us (68%)
  local copies, waits for them, and re-layouts  10.1 us (13%)
  other arithmetic  7.02 us (9%)
  starting transfers between devices  6.55 us (8%)
  between operations  0.79 us (1%)
    pallas_call x1, Pallas kernels, project(): pl.pallas_call(functools.partial(project_kernel, ranks), out_shape=(out,...  33.4 us
    pallas_call x1, Pallas kernels, attend(): pl.pallas_call(functools.partial(attend_kernel, dims), out_shape=jax.Shap...  12.6 us
    ppermute x3, starting transfers between devices, per_device(): lax.ppermute(block, 'replica', [(r, (r + d) % replicas) for r in range(re...  6.55 us
    pallas_call x1, Pallas kernels, pack(): pl.pallas_call(functools.partial(pack_kernel, blocks, head_dim), out_shap...  3.98 us
    unnamed x21, local copies, waits for them, and re-layouts  3.64 us
    convert_element_type x1, other arithmetic, per_device(): normed = (hidden.astype(jnp.float32) * scale * gain).astype(jnp.bfloat16)  3.5 us
    pallas_call x1, Pallas kernels, attend_moved(): pl.pallas_call(functools.partial(moved_kernel, dims), out_shape=jax.Shape...  2.86 us
    reshape x2, local copies, waits for them, and re-layouts, per_device(): head_out.reshape(slots, steps, heads * head_dim).transpose(1, 0, 2)  2.12 us
  transfers between devices with their start and end apart: 3, of which 0 were waited for; matrix products, arithmetic and copies ran while one was open for 5% of the time, Pallas kernels for 16%

profile of v3, /device:TPU:0, one launch (start us, length us, event | category | flops | bytes accessed | tf_op | source)
XLA Modules:
  0.0 77.3 jit_solution(13341850533605834614)
XLA Ops:
  0.7 1.0 %slice_reduce_fusion = (s32[4]{0:T(128)S(1)}, s32[4]{0:T(128)S(1)}, s32[4]{0:T(128)S(1)}, s32[4]{0:T(128)S(1)}) fusion(s32[4,4]{1,0:T(4,128)} %param.14), kind=kLoop, calls=%fused_computation.10 | loop fusion | bytes 128 | tf_op jit(solution)/shard_map/slice | solution.py:382
  1.7 0.8 %copy.22 = s32[64,10]{1,0:T(8,128)S(1)} copy(s32[64,10]{0,1:T(8,128)} %param.13) | data formatting | bytes 5120 | tf_op args[4]
  2.5 0.7 reshape.103.table_ref
  3.2 0.2 select_reduce_fusion.1.chosen_ref
  3.4 0.0 copy-start.7
  3.4 1.3 %select_reduce_fusion.size_ref = s32[3]{0:T(128)} fusion(s32[64]{0:T(128)} %count_ref.1, s32[3]{0:T(128)S(1)} %select_reduce_fusion.1.chosen_ref), kind=kLoop, calls=%fused_computation.7 | loop fusion | flops 573 | bytes 280 | tf_op jit(solution)/shard_map/reduce_sum | solution.py:389
  4.8 0.0 copy-done.7
  4.8 0.0 copy-start.6
  4.8 0.0 copy-start.8
  4.8 0.0 copy-start.5
  4.8 0.0 copy-start.1
  4.8 4.0 %shard_map.105 = (bf16[11,32,256]{2,1,0:T(8,128)(2,1)}, bf16[11,32,256]{2,1,0:T(8,128)(2,1)}, bf16[11,32,256]{2,1,0:T(8,128)(2,1)}) custom-call(s32[640]{0:T(1024)} %reshape.103.table_ref, s32[3]{0:T(128)} %copy-done.7, s32[3]{0:T(128)} %select_reduce_fusion.size_ref, bf16[640,16,2,256]{3,2,1,0:T(2,128)(2,1)} %pool_ref.3), custom_call_target="tpu_custom_call" | custom-call | tf_op jit(solution)/shard_map/pallas_call | solution.py:181
  8.8 3.2 %collective-permute-start = (bf16[11,32,256]{2,1,0:T(8,128)(2,1)}, bf16[11,32,256]{2,1,0:T(8,128)(2,1)S(1)}, u32[]{:S(2)}, u32[]{:S(2)}) collective-permute-start(bf16[11,32,256]{2,1,0:T(8,128)(2,1)} %get-tuple-element.7), channel_id=1, source_target_pairs={{0,4},{4,8},{8,12},{12,0},{1,5},{5,9},{9,13},{13,1},{2,6},{6,10},{... | collective-permute-start | bytes 540680 | tf_op jit(solution)/shard_map/ppermute | solution.py:392
  12.0 2.1 %collective-permute-start.1 = (bf16[11,32,256]{2,1,0:T(8,128)(2,1)}, bf16[11,32,256]{2,1,0:T(8,128)(2,1)S(1)}, u32[]{:S(2)}, u32[]{:S(2)}) collective-permute-start(bf16[11,32,256]{2,1,0:T(8,128)(2,1)} %get-tuple-element.8), channel_id=1, source_target_pairs={{0,8},{4,12},{8,0},{12,4},{1,9},{5,13},{9,1},{13,5},{2,10},{6,14},... | collective-permute-start | bytes 540680 | tf_op jit(solution)/shard_map/ppermute | solution.py:392
  14.1 1.2 %collective-permute-start.2 = (bf16[11,32,256]{2,1,0:T(8,128)(2,1)}, bf16[11,32,256]{2,1,0:T(8,128)(2,1)S(1)}, u32[]{:S(2)}, u32[]{:S(2)}) collective-permute-start(bf16[11,32,256]{2,1,0:T(8,128)(2,1)} %get-tuple-element.9), channel_id=1, source_target_pairs={{0,12},{4,0},{8,4},{12,8},{1,13},{5,1},{9,5},{13,9},{2,14},{6,2},{... | collective-permute-start | bytes 540680 | tf_op jit(solution)/shard_map/ppermute | solution.py:392
  15.3 0.1 fusion.1
  15.4 0.0 copy-done.6
  15.4 0.0 copy-done.8
  15.5 0.8 convert_element_type.21.keep_ref
  16.2 0.0 copy-done.5
  16.2 0.1 copy.21
  16.3 0.1 reshape.102
  16.4 0.0 copy-done.1
  16.4 0.1 copy.25
  16.5 0.8 %copy.20 = bf16[2,64,16,128]{3,2,0,1:T(8,128)(2,1)} copy(bf16[2,64,16,128]{3,2,1,0:T(8,128)(2,1)S(1)} %bitcast.20) | data formatting | bytes 1048576 | tf_op jit(solution)/shard_map/reshape | solution.py:396
  17.4 0.2 select_reduce_fusion.2
  17.6 0.8 %pad.4.fresh_ref = bf16[64,16,256]{2,1,0:T(8,128)(2,1)} pad(bf16[64,4,256]{2,1,0:T(4,128)(2,1)S(1)} %reshape.102, bf16[]{:T(256)} %constant.34.clone.1), padding=0_0x0_12x0_0 | pad | bytes 655362 | tf_op jit(solution)/shard_map/jit(_pad)/pad | solution.py:399
  18.4 12.6 %shard_map.104.main_ref = bf16[64,32,128]{2,1,0:T(8,128)(2,1)} custom-call(s32[640]{0:T(1024)} %reshape.103.table_ref, s32[64]{0:T(128)} %count_ref.1, bf16[64,32,128]{2,1,0:T(8,128)(2,1)} %bitcast.15, bf16[64,16,256]{2,1,0:T(8,128)(2,1)} %pad.4.fresh_ref, bf16[640,16,2,256]{3,2,1,0:T(2,128)(2,1)} %pool_ref.3), custom_call_target="tpu_custom_call" | custom-call | flops 352321536 | bytes 20971520 | tf_op jit(solution)/shard_map/pallas_call | solution.py:90
  31.1 0.6 broadcast_add_fusion.slot_ref
  31.6 0.0 collective-permute-done.refs_0_
  31.7 0.0 copy-start.2
  31.7 0.0 collective-permute-done.1.refs_1_
  31.7 0.0 copy-start.3
  31.7 0.0 collective-permute-done.2.refs_2_
  31.7 0.6 copy-done.2
  32.3 0.1 copy-done.3
  32.4 0.0 copy-start.4
  32.4 0.7 copy-done.4
  33.1 2.9 %shard_map.106 = bf16[64,32,128]{2,1,0:T(8,128)(2,1)} custom-call(s32[3]{0:T(128)} %broadcast_add_fusion.slot_ref, bf16[64,32,128]{2,1,0:T(8,128)(2,1)} %bitcast.16, bf16[64,16,256]{2,1,0:T(8,128)(2,1)} %pad.4.fresh_ref, bf16[64,32,128]{2,1,0:T(8,128)(2,1)} %shard_map.104.main_ref, bf16[11,32,256]{2,1,0:T(8,128)(2,1)} %copy-done.2, ...), custom_call_target="tpu_custom_call" | custom-call | tf_op jit(solution)/shard_map/pallas_call | solution.py:143
  35.9 1.2 %reshape.104 = bf16[64,2,2048]{2,1,0:T(2,128)(2,1)S(1)} reshape(bf16[64,32,128]{2,1,0:T(8,128)(2,1)} %shard_map.106) | data formatting | bytes 1048576 | tf_op jit(solution)/shard_map/reshape | solution.py:405
  37.1 1.0 %copy.23 = bf16[64,2,2048]{2,0,1:T(8,128)(2,1)} copy(bf16[64,2,2048]{2,1,0:T(2,128)(2,1)S(1)} %reshape.104) | data formatting | bytes 1048576 | tf_op jit(solution)/shard_map/reshape | solution.py:405
  38.1 33.4 %shard_map.107 = (bf16[128,8192]{1,0:T(8,128)(2,1)}, f32[128,1]{1,0:T(8,128)}) custom-call(bf16[128,2048]{1,0:T(8,128)(2,1)} %bitcast.17, f32[128,1]{1,0:T(8,128)} %convert_element_type.21.keep_ref, bf16[128,8192]{1,0:T(8,128)(2,1)} %bitcast.18, bf16[2048,8192]{1,0:T(8,128)(2,1)} %w_ref.1), custom_call_target="tpu_custom_call" | custom-call | flops 4294967296 | bytes 33554432 | tf_op jit(solution)/shard_map/pallas_call | solution.py:347
  71.4 0.0 copy-start
  71.4 1.1 %reduce.4 = f32[128]{0:T(128)S(1)} reduce(f32[128,1]{1,0:T(8,128)} %get-tuple-element.11, f32[]{:T(128)} %constant.44), dimensions={1}, to_apply=%get-tuple-element.11.reduce_sub_computation | reduce | bytes 1028 | tf_op jit(solution)/shard_map/pallas_call | solution.py:347
  72.5 3.5 %multiply_convert_fusion = bf16[128,8192]{1,0:T(8,128)(2,1)} fusion(bf16[128,8192]{1,0:T(8,128)(2,1)} %get-tuple-element.10, f32[8192]{0:T(1024)S(1)} %convert_element_type.19, f32[128]{0:T(128)S(1)} %reduce.4), kind=kLoop, calls=%fused_computation | loop fusion | flops 4194304 | bytes 4227584 | tf_op jit(solution)/shard_map/convert_element_type | solution.py:415
  76.0 0.0 copy-done
  76.0 1.3 %copy.27 = bf16[2,64,8192]{2,1,0:T(8,128)(2,1)} copy(bf16[2,64,8192]{2,1,0:T(8,128)(2,1)S(1)} %bitcast.14) | data formatting | bytes 4194304
  (7 shorter events, 0.0 us)
Async XLA Ops:
  3.4 1.4 %copy-start.7 = (s32[3]{0:T(128)}, s32[3]{0:T(128)S(1)}, u32[]{:S(2)}) copy-start(s32[3]{0:T(128)S(1)} %select_reduce_fusion.1.chosen_ref) | copy-start | bytes 40
  4.8 10.7 %copy-start.6 = (bf16[8192]{0:T(1024)(128)(2,1)S(1)}, bf16[8192]{0:T(1024)(128)(2,1)}, u32[]{:S(2)}) copy-start(bf16[8192]{0:T(1024)(128)(2,1)} %param.17) | copy-start | bytes 49156
  4.8 10.7 %copy-start.8 = (s32[64]{0:T(128)S(1)}, s32[64]{0:T(128)}, u32[]{:S(2)}) copy-start(s32[64]{0:T(128)} %count_ref.1) | copy-start | bytes 772
  4.8 11.5 %copy-start.5 = (bf16[2,64,2,256]{3,2,1,0:T(2,128)(2,1)S(1)}, bf16[2,64,2,256]{3,2,1,0:T(2,128)(2,1)}, u32[]{:S(2)}) copy-start(bf16[2,64,2,256]{3,2,1,0:T(2,128)(2,1)} %param.10) | copy-start | bytes 393220
  4.8 11.6 %copy-start.1 = (bf16[2,64,2048]{2,1,0:T(8,128)(2,1)S(1)}, bf16[2,64,2048]{2,1,0:T(8,128)(2,1)}, u32[]{:S(2)}) copy-start(bf16[2,64,2048]{2,1,0:T(8,128)(2,1)} %param.9) | copy-start | bytes 1572868
  8.8 22.9 %collective-permute-start = (bf16[11,32,256]{2,1,0:T(8,128)(2,1)}, bf16[11,32,256]{2,1,0:T(8,128)(2,1)S(1)}, u32[]{:S(2)}, u32[]{:S(2)}) collective-permute-start(bf16[11,32,256]{2,1,0:T(8,128)(2,1)} %get-tuple-element.7), channel_id=1, source_target_pairs={{0,4},{4,8},{8,12},{12,0},{1,5},{5,9},{9,13},{13,1},{2,6},{6,10},{... | collective-permute-start | bytes 540680 | tf_op jit(solution)/shard_map/ppermute | solution.py:392
  12.0 19.7 %collective-permute-start.1 = (bf16[11,32,256]{2,1,0:T(8,128)(2,1)}, bf16[11,32,256]{2,1,0:T(8,128)(2,1)S(1)}, u32[]{:S(2)}, u32[]{:S(2)}) collective-permute-start(bf16[11,32,256]{2,1,0:T(8,128)(2,1)} %get-tuple-element.8), channel_id=1, source_target_pairs={{0,8},{4,12},{8,0},{12,4},{1,9},{5,13},{9,1},{13,5},{2,10},{6,14},... | collective-permute-start | bytes 540680 | tf_op jit(solution)/shard_map/ppermute | solution.py:392
  14.1 17.6 %collective-permute-start.2 = (bf16[11,32,256]{2,1,0:T(8,128)(2,1)}, bf16[11,32,256]{2,1,0:T(8,128)(2,1)S(1)}, u32[]{:S(2)}, u32[]{:S(2)}) collective-permute-start(bf16[11,32,256]{2,1,0:T(8,128)(2,1)} %get-tuple-element.9), channel_id=1, source_target_pairs={{0,12},{4,0},{8,4},{12,8},{1,13},{5,1},{9,5},{13,9},{2,14},{6,2},{... | collective-permute-start | bytes 540680 | tf_op jit(solution)/shard_map/ppermute | solution.py:392
  31.7 0.7 copy-start.2
  31.7 0.7 copy-start.3
  32.4 0.7 copy-start.4
  71.4 4.6 %copy-start = (bf16[128,8192]{1,0:T(8,128)(2,1)S(1)}, bf16[128,8192]{1,0:T(8,128)(2,1)}, u32[]{:S(2)}) copy-start(bf16[128,8192]{1,0:T(8,128)(2,1)} %get-tuple-element.10) | copy-start | bytes 6291460

commit v4 on v3

--- a/solution.py
+++ b/solution.py
@@ -58,7 +58,7 @@
     get_values.wait()
 
     def rows_of(store, new, n):
-        found = [store[table_ref[n * blocks + b]].reshape(block_rows, head_dim) for b in range(blocks)]
+        found = [store[table_ref[n, b]].reshape(block_rows, head_dim) for b in range(blocks)]
         return jnp.concatenate(found + [new], axis=0)
 
     def body(i, carry):
@@ -101,7 +101,7 @@
         cost_estimate=pl.CostEstimate(
             flops=4 * slots * rows * 336 * head_dim, bytes_accessed=4 * pool.size, transcendentals=slots * rows * 336
         ),
-    )(table.reshape(-1), count, query_rows, fresh_rows, pool)
+    )(table, count, query_rows, fresh_rows, pool)
 
 
 def moved_kernel(dims, slot_ref, query_ref, fresh_ref, main_ref, *refs):
@@ -154,14 +154,14 @@
     for j in range(len(out_refs)):
         for b in range(blocks):
             at = j * blocks + b
-            block = pool_ref.at[table_ref[chosen_ref[j] * blocks + b]]
+            block = pool_ref.at[table_ref[chosen_ref[j], b]]
             for half, store in enumerate((keys, values)):
                 part = block.at[..., pl.ds(half * head_dim, head_dim)]
                 copies.append(pltpu.make_async_copy(part, store.at[at], sems.at[2 * at + half]))
                 copies[-1].start()
     shape = out_refs[0].shape[1:]
     for j, out_ref in enumerate(out_refs):
-        size = jnp.full(shape, size_ref[j], jnp.int32)
+        size = jnp.full(shape, size_ref[chosen_ref[j]], jnp.int32)
         out_ref[blocks] = size.astype(jnp.float32).astype(jnp.bfloat16)
     for copy in copies:
         copy.wait()
@@ -189,13 +189,14 @@
             pltpu.SemaphoreType.DMA((2 * moves * blocks,)),
         ],
         compiler_params=pltpu.CompilerParams(vmem_limit_bytes=VMEM_ASK),
-    )(table.reshape(-1), chosen, sizes, pool)
+    )(table, chosen, sizes, pool)
 
 
 def project_kernel(ranks, head_ref, keep_ref, resid_ref, w_ref, hidden_ref, scale_ref,
                    weight, sib_out, sib_in, y_out, y_in, whole, w_sem, s_send, s_recv, y_send, y_recv,
-                   g_send, g_recv, h_send, h_recv):
+                   g_send, g_recv, h_send, h_recv, resid_here, resid_sem, out_sem):
     rows, width = hidden_ref.shape
+    get_resid = pltpu.make_async_copy(resid_ref, resid_here, resid_sem.at[0])
     tall = ranks // 2
     pieces = width // ranks // CHUNK
     me = lax.axis_index("tensor")
@@ -231,6 +232,7 @@
         return carry
 
     lax.fori_loop(0, steps, start_fetch, 0)
+    get_resid.start()
     pl.semaphore_wait(barrier, tall)
 
     def to_sibling(i):
@@ -283,6 +285,8 @@
 
     lax.fori_loop(0, steps - pieces, far, 0)
 
+    get_resid.wait()
+
     def near(k, carry):
         mixed = products(steps - pieces + k)
         for off in range(1, tall):
@@ -291,7 +295,7 @@
             mixed = mixed + y_in[at].astype(jnp.float32)
         slot = place(core, level, k)
         cols = pl.ds(pl.multiple_of(slot * CHUNK, CHUNK), CHUNK)
-        total = resid_ref[:, cols].astype(jnp.float32) + mixed
+        total = resid_here[:, cols].astype(jnp.float32) + mixed
         whole[slot] = jnp.where(keep_ref[...] > 0.0, total, 0.0).astype(jnp.bfloat16)
         for off in range(1, tall):
             gather_peer(off, k).start()
@@ -322,8 +326,12 @@
             copy.wait_recv()
             squares = squares + square(slot)
     scale_ref[...] = lax.rsqrt(squares * (1.0 / width) + 1e-05)
-    for j in range(width // CHUNK):
-        hidden_ref[:, pl.ds(j * CHUNK, CHUNK)] = whole[j]
+    stores = [
+        pltpu.make_async_copy(whole.at[j], hidden_ref.at[:, pl.ds(j * CHUNK, CHUNK)], out_sem.at[j])
+        for j in range(width // CHUNK)
+    ]
+    for store in stores:
+        store.start()
     for i in range(steps):
         to_sibling(i).wait_send()
     for i in range(steps - pieces):
@@ -333,6 +341,8 @@
         for off in range(1, tall):
             gather_peer(off, k).wait_send()
             hand_over(core, off, k)[1].wait_send()
+    for store in stores:
+        store.wait()
 
 
 def project(flat_heads, keep_rows, resid_rows, w_out, ranks):
@@ -347,8 +357,8 @@
     return pl.pallas_call(
         functools.partial(project_kernel, ranks),
         out_shape=(out, jax.ShapeDtypeStruct((rows, 1), jnp.float32)),
-        in_specs=[VMEM, VMEM, VMEM, ANY],
-        out_specs=(VMEM, VMEM),
+        in_specs=[VMEM, VMEM, ANY, ANY],
+        out_specs=(ANY, VMEM),
         scratch_shapes=[
             pltpu.VMEM((2 * steps, depth, CHUNK), jnp.bfloat16),
             pltpu.VMEM((steps,) + block, jnp.bfloat16),
@@ -361,6 +371,7 @@
             dma((far,)), dma((far,)),
             dma((far,)), dma((far,)),
             dma((steps,)), dma((steps,)),
+            pltpu.VMEM((rows, width), jnp.bfloat16), dma((1,)), dma((2 * steps,)),
         ],
         compiler_params=pltpu.CompilerParams(
             collective_id=0, has_side_effects=True, vmem_limit_bytes=56 * 2**20
@@ -369,6 +380,27 @@
             flops=2 * rows * depth * width, bytes_accessed=2 * depth * width, transcendentals=0
         ),
     )(flat_heads, keep_rows, resid_rows, w_out)
+
+
+def norm_kernel(hidden_ref, scale_ref, gain_ref, same_ref, normed_ref):
+    hidden = hidden_ref[...]
+    same_ref[...] = hidden
+    gain = gain_ref[...].astype(jnp.float32)
+    normed_ref[...] = (hidden.astype(jnp.float32) * scale_ref[...] * gain).astype(jnp.bfloat16)
+
+
+def norm(hidden, scale, gain):
+    rows, width = hidden.shape
+    cols = 1024
+    block = pl.BlockSpec((rows, cols), lambda i: (0, i))
+    out = jax.ShapeDtypeStruct((rows, width), jnp.bfloat16)
+    return pl.pallas_call(
+        norm_kernel,
+        grid=(width // cols,),
+        out_shape=(out, out),
+        in_specs=[block, pl.BlockSpec((rows, 1), lambda i: (0, 0)), pl.BlockSpec((1, cols), lambda i: (0, i))],
+        out_specs=(block, block),
+    )(hidden, scale, gain)
 
 
 def per_device(replicas, ranks, queries, new_kv, pool, lengths, block_table, plan, w_out, residual, norm_gain):
@@ -386,11 +418,10 @@
     shifts = jnp.arange(1, replicas, dtype=jnp.int32)
     leaving = sending[None, :] & (target[None, :] == ((my_replica + shifts) % replicas)[:, None])
     chosen = jnp.sum(jnp.where(leaving, source_slot[None, :], 0), axis=1)
-    sizes = jnp.sum(jnp.where(slot_ids[None, :] == chosen[:, None], lengths[None, :], 0), axis=1)
     pool = drop_single(pool)
     got = [
         lax.ppermute(block, "replica", [(r, (r + d) % replicas) for r in range(replicas)])
-        for d, block in enumerate(pack(pool, block_table, chosen, sizes, copies), 1)
+        for d, block in enumerate(pack(pool, block_table, chosen, lengths, copies), 1)
     ]
 
     query_rows = queries.reshape(steps, slots, heads, head_dim).transpose(1, 0, 2, 3)
@@ -411,8 +442,7 @@
     keep_rows = jnp.tile(live, steps)[:, None].astype(jnp.float32)
     resid_rows = residual.reshape(steps * slots, width)
     hidden, scale = project(flat_heads, keep_rows, resid_rows, w_out, ranks)
-    gain = norm_gain.astype(jnp.float32)[None, :]
-    normed = (hidden.astype(jnp.float32) * scale * gain).astype(jnp.bfloat16)
+    hidden, normed = norm(hidden, scale, norm_gain[None, :])
     out_shape = (steps, slots, width)
     return (hidden.reshape(out_shape), normed.reshape(out_shape))
 

time: 77.8 us -> 78.2 us (level)
  Pallas kernels: 52.8 us -> 59.3 us
  other arithmetic: 7.02 us -> 1.57 us
  local copies, waits for them, and re-layouts: 10.1 us -> 9.31 us
    pallas_call x0 -> x1, Pallas kernels: none -> 6.11 us  [norm(): pl.pallas_call(norm_kernel, grid=(width // cols,), out_shape=(out, out),...]
    convert_element_type x2 -> x0, other arithmetic: 3.5 us -> none  [the longest x1 3.5 us: per_device(): normed = (hidden.astype(jnp.float32) * scale * gain).astype(jnp.bfloat16)]
    reduce_sum x1 -> x0, other arithmetic: 1.35 us -> none  [per_device(): jnp.sum(jnp.where(slot_ids[None, :] == chosen[:, None], lengths[None, :],...]
    pallas_call x1 -> x0, other arithmetic: 1.09 us -> none  [project(): pl.pallas_call(functools.partial(project_kernel, ranks), out_shape=(out,...]
    unnamed x21 -> x16, local copies, waits for them, and re-layouts: 3.64 us -> 2.91 us
where the time goes in v4:
time: 78.2 us; the launch traced here: 77.4 us
  Pallas kernels  59.3 us (76%)
  local copies, waits for them, and re-layouts  9.31 us (12%)
  starting transfers between devices  6.44 us (8%)
  other arithmetic  1.57 us (2%)
    pallas_call x1, Pallas kernels, project(): pl.pallas_call(functools.partial(project_kernel, ranks), out_shape=(out,...  33.1 us
    pallas_call x1, Pallas kernels, attend(): pl.pallas_call(functools.partial(attend_kernel, dims), out_shape=jax.Shap...  12.7 us
    ppermute x3, starting transfers between devices, per_device(): lax.ppermute(block, 'replica', [(r, (r + d) % replicas) for r in range(re...  6.44 us
    pallas_call x1, Pallas kernels, norm(): pl.pallas_call(norm_kernel, grid=(width // cols,), out_shape=(out, out),...  6.11 us
    pallas_call x1, Pallas kernels, pack(): pl.pallas_call(functools.partial(pack_kernel, blocks, head_dim), out_shap...  4.58 us
    unnamed x16, local copies, waits for them, and re-layouts  2.91 us
    pallas_call x1, Pallas kernels, attend_moved(): pl.pallas_call(functools.partial(moved_kernel, dims), out_shape=jax.Shape...  2.86 us
    reshape x2, local copies, waits for them, and re-layouts, per_device(): head_out.reshape(slots, steps, heads * head_dim).transpose(1, 0, 2)  2.12 us
  transfers between devices with their start and end apart: 3, of which 0 were waited for; matrix products, arithmetic and copies ran while one was open for 5% of the time, Pallas kernels for 16%

profile of v4, /device:TPU:0, one launch (start us, length us, event | category | flops | bytes accessed | tf_op | source)
XLA Modules:
  0.0 77.4 jit_solution(17181276224826841023)
XLA Ops:
  0.7 1.0 %slice_reduce_fusion = (s32[4]{0:T(128)S(1)}, s32[4]{0:T(128)S(1)}, s32[4]{0:T(128)S(1)}, s32[4]{0:T(128)S(1)}) fusion(s32[4,4]{1,0:T(4,128)} %param.14), kind=kLoop, calls=%fused_computation.7 | loop fusion | bytes 128 | tf_op jit(solution)/shard_map/slice | solution.py:414
  1.7 1.4 %copy.19.table_ref = s32[64,10]{1,0:T(8,128)} copy(s32[64,10]{0,1:T(8,128)} %param.13) | data formatting | bytes 5120 | tf_op args[4]
  3.1 0.7 select_reduce_fusion.chosen_ref
  3.8 0.0 copy-start.5
  3.8 0.0 copy-start.6
  3.8 0.0 copy-start.4
  3.8 0.0 copy-start
  3.8 4.6 %shard_map.105 = (bf16[11,32,256]{2,1,0:T(8,128)(2,1)}, bf16[11,32,256]{2,1,0:T(8,128)(2,1)}, bf16[11,32,256]{2,1,0:T(8,128)(2,1)}) custom-call(s32[64,10]{1,0:T(8,128)} %copy.19.table_ref, s32[3]{0:T(128)} %select_reduce_fusion.chosen_ref, s32[64]{0:T(128)} %size_ref.1, bf16[640,16,2,256]{3,2,1,0:T(2,128)(2,1)} %pool_ref.3), custom_call_target="tpu_custom_call" | custom-call | tf_op jit(solution)/shard_map/pallas_call | solution.py:181
  8.4 2.6 %collective-permute-start = (bf16[11,32,256]{2,1,0:T(8,128)(2,1)}, bf16[11,32,256]{2,1,0:T(8,128)(2,1)S(1)}, u32[]{:S(2)}, u32[]{:S(2)}) collective-permute-start(bf16[11,32,256]{2,1,0:T(8,128)(2,1)} %get-tuple-element.9), channel_id=1, source_target_pairs={{0,4},{4,8},{8,12},{12,0},{1,5},{5,9},{9,13},{13,1},{2,6},{6,10},{... | collective-permute-start | bytes 540680 | tf_op jit(solution)/shard_map/ppermute | solution.py:423
  10.9 3.1 %collective-permute-start.1 = (bf16[11,32,256]{2,1,0:T(8,128)(2,1)}, bf16[11,32,256]{2,1,0:T(8,128)(2,1)S(1)}, u32[]{:S(2)}, u32[]{:S(2)}) collective-permute-start(bf16[11,32,256]{2,1,0:T(8,128)(2,1)} %get-tuple-element.10), channel_id=1, source_target_pairs={{0,8},{4,12},{8,0},{12,4},{1,9},{5,13},{9,1},{13,5},{2,10},{6,14},... | collective-permute-start | bytes 540680 | tf_op jit(solution)/shard_map/ppermute | solution.py:423
  14.1 0.7 collective-permute-start.2
  14.8 0.1 fusion.1
  14.9 0.0 copy-done.5
  14.9 0.6 broadcast_in_dim.35.gain_ref
  15.6 0.0 copy-done.6
  15.6 0.8 convert_element_type.9.keep_ref
  16.3 0.0 copy-done.4
  16.3 0.1 copy.18
  16.4 0.1 reshape.95
  16.5 0.0 copy-done
  16.5 0.1 copy.23
  16.6 0.8 %copy.17 = bf16[2,64,16,128]{3,2,0,1:T(8,128)(2,1)} copy(bf16[2,64,16,128]{3,2,1,0:T(8,128)(2,1)S(1)} %bitcast.18) | data formatting | bytes 1048576 | tf_op jit(solution)/shard_map/reshape | solution.py:427
  17.5 0.2 select_reduce_fusion.1
  17.7 0.8 %pad.4.fresh_ref = bf16[64,16,256]{2,1,0:T(8,128)(2,1)} pad(bf16[64,4,256]{2,1,0:T(4,128)(2,1)S(1)} %reshape.95, bf16[]{:T(256)} %constant.34.clone.1), padding=0_0x0_12x0_0 | pad | bytes 655362 | tf_op jit(solution)/shard_map/jit(_pad)/pad | solution.py:430
  18.5 12.7 %shard_map.104.main_ref = bf16[64,32,128]{2,1,0:T(8,128)(2,1)} custom-call(s32[64,10]{1,0:T(8,128)} %copy.19.table_ref, s32[64]{0:T(128)} %size_ref.1, bf16[64,32,128]{2,1,0:T(8,128)(2,1)} %bitcast.14, bf16[64,16,256]{2,1,0:T(8,128)(2,1)} %pad.4.fresh_ref, bf16[640,16,2,256]{3,2,1,0:T(2,128)(2,1)} %pool_ref.3), custom_call_target="tpu_custom_call" | custom-call | flops 352321536 | bytes 20971520 | tf_op jit(solution)/shard_map/pallas_call | solution.py:90
  31.2 0.6 broadcast_add_fusion.slot_ref
  31.7 0.0 collective-permute-done.refs_0_
  31.7 0.0 copy-start.1
  31.7 0.0 collective-permute-done.1.refs_1_
  31.7 0.0 copy-start.2
  31.8 0.0 collective-permute-done.2.refs_2_
  31.8 0.6 copy-done.1
  32.4 0.1 copy-done.2
  32.5 0.0 copy-start.3
  32.5 0.7 copy-done.3
  33.2 2.9 %shard_map.106 = bf16[64,32,128]{2,1,0:T(8,128)(2,1)} custom-call(s32[3]{0:T(128)} %broadcast_add_fusion.slot_ref, bf16[64,32,128]{2,1,0:T(8,128)(2,1)} %bitcast.15, bf16[64,16,256]{2,1,0:T(8,128)(2,1)} %pad.4.fresh_ref, bf16[64,32,128]{2,1,0:T(8,128)(2,1)} %shard_map.104.main_ref, bf16[11,32,256]{2,1,0:T(8,128)(2,1)} %copy-done.1, ...), custom_call_target="tpu_custom_call" | custom-call | tf_op jit(solution)/shard_map/pallas_call | solution.py:143
  36.0 1.2 %reshape.96 = bf16[64,2,2048]{2,1,0:T(2,128)(2,1)S(1)} reshape(bf16[64,32,128]{2,1,0:T(8,128)(2,1)} %shard_map.106) | data formatting | bytes 1048576 | tf_op jit(solution)/shard_map/reshape | solution.py:436
  37.2 1.0 %copy.21 = bf16[64,2,2048]{2,0,1:T(8,128)(2,1)} copy(bf16[64,2,2048]{2,1,0:T(2,128)(2,1)S(1)} %reshape.96) | data formatting | bytes 1048576 | tf_op jit(solution)/shard_map/reshape | solution.py:436
  38.1 33.1 %shard_map.107 = (bf16[128,8192]{1,0:T(8,128)(2,1)}, f32[128,1]{1,0:T(8,128)}) custom-call(bf16[128,2048]{1,0:T(8,128)(2,1)} %bitcast.16, f32[128,1]{1,0:T(8,128)} %convert_element_type.9.keep_ref, bf16[128,8192]{1,0:T(8,128)(2,1)} %bitcast.17, bf16[2048,8192]{1,0:T(8,128)(2,1)} %w_ref.1), custom_call_target="tpu_custom_call" | custom-call | flops 4294967296 | bytes 33554432 | tf_op jit(solution)/shard_map/pallas_call | solution.py:357
  71.2 6.1 %shard_map.108 = (bf16[128,8192]{1,0:T(8,128)(2,1)}, bf16[128,8192]{1,0:T(8,128)(2,1)}) custom-call(bf16[128,8192]{1,0:T(8,128)(2,1)} %get-tuple-element.12.hidden_ref, f32[128,1]{1,0:T(8,128)} %get-tuple-element.13.scale_ref, bf16[1,8192]{1,0:T(2,128)(2,1)} %broadcast_in_dim.35.gain_ref), custom_call_target="tpu_custom_call" | custom-call | tf_op jit(solution)/shard_map/pallas_call | solution.py:397
  (6 shorter events, 0.0 us)
Async XLA Ops:
  3.8 11.1 %copy-start.5 = (bf16[8192]{0:T(1024)(128)(2,1)S(1)}, bf16[8192]{0:T(1024)(128)(2,1)}, u32[]{:S(2)}) copy-start(bf16[8192]{0:T(1024)(128)(2,1)} %param.17) | copy-start | bytes 49156
  3.8 11.8 %copy-start.6 = (s32[64]{0:T(128)S(1)}, s32[64]{0:T(128)}, u32[]{:S(2)}) copy-start(s32[64]{0:T(128)} %size_ref.1) | copy-start | bytes 772
  3.8 12.5 %copy-start.4 = (bf16[2,64,2,256]{3,2,1,0:T(2,128)(2,1)S(1)}, bf16[2,64,2,256]{3,2,1,0:T(2,128)(2,1)}, u32[]{:S(2)}) copy-start(bf16[2,64,2,256]{3,2,1,0:T(2,128)(2,1)} %param.10) | copy-start | bytes 393220
  3.8 12.7 %copy-start = (bf16[2,64,2048]{2,1,0:T(8,128)(2,1)S(1)}, bf16[2,64,2048]{2,1,0:T(8,128)(2,1)}, u32[]{:S(2)}) copy-start(bf16[2,64,2048]{2,1,0:T(8,128)(2,1)} %param.9) | copy-start | bytes 1572868
  8.4 23.4 %collective-permute-start = (bf16[11,32,256]{2,1,0:T(8,128)(2,1)}, bf16[11,32,256]{2,1,0:T(8,128)(2,1)S(1)}, u32[]{:S(2)}, u32[]{:S(2)}) collective-permute-start(bf16[11,32,256]{2,1,0:T(8,128)(2,1)} %get-tuple-element.9), channel_id=1, source_target_pairs={{0,4},{4,8},{8,12},{12,0},{1,5},{5,9},{9,13},{13,1},{2,6},{6,10},{... | collective-permute-start | bytes 540680 | tf_op jit(solution)/shard_map/ppermute | solution.py:423
  10.9 20.8 %collective-permute-start.1 = (bf16[11,32,256]{2,1,0:T(8,128)(2,1)}, bf16[11,32,256]{2,1,0:T(8,128)(2,1)S(1)}, u32[]{:S(2)}, u32[]{:S(2)}) collective-permute-start(bf16[11,32,256]{2,1,0:T(8,128)(2,1)} %get-tuple-element.10), channel_id=1, source_target_pairs={{0,8},{4,12},{8,0},{12,4},{1,9},{5,13},{9,1},{13,5},{2,10},{6,14},... | collective-permute-start | bytes 540680 | tf_op jit(solution)/shard_map/ppermute | solution.py:423
  14.1 17.7 %collective-permute-start.2 = (bf16[11,32,256]{2,1,0:T(8,128)(2,1)}, bf16[11,32,256]{2,1,0:T(8,128)(2,1)S(1)}, u32[]{:S(2)}, u32[]{:S(2)}) collective-permute-start(bf16[11,32,256]{2,1,0:T(8,128)(2,1)} %get-tuple-element.11), channel_id=1, source_target_pairs={{0,12},{4,0},{8,4},{12,8},{1,13},{5,1},{9,5},{13,9},{2,14},{6,2},{... | collective-permute-start | bytes 540680 | tf_op jit(solution)/shard_map/ppermute | solution.py:423
  31.7 0.7 copy-start.1
  31.7 0.7 copy-start.2
  32.5 0.7 copy-start.3
